TPU v7x, 512 devices: a whole 4x4x16 slice. The times are simulated.
512 devices in a mesh: lat: 32 (over x, z_hi, core), lon: 16 (over z_lo, y).
Axes of the slice: x: 4, y: 4, z: 16 (z_hi: 4, z_lo: 4; z = z_hi * 4 + z_lo), core: 2. Of those that a mesh axis runs over, the one named last changes fastest.
Arguments:
- cotangent: bfloat16 [3, 50, 1536, 4096], P(None, None, 'lat', 'lon'), may hold values from -6 to 6
- wave_order: int32 [512], replicated, may hold values from 0 to 511, each once
- band_diagonal: bfloat16 [512, 24, 4096], P(('lat', 'lon')), may hold values from -0.4375 to 0.4375
- band_lower: bfloat16 [512, 23, 4096], P(('lat', 'lon')), may hold values from -0.4375 to 0.4375
- vertical_matrix: bfloat16 [3, 50, 50], replicated, may hold values from -0.875 to 0.875
Outputs:
- adjoint_spectra: bfloat16 [512, 2, 3, 50, 1536], P(('lat', 'lon'))
Inputs may be any that keep to these rules, and one draw needn't show every extreme that they name: `wave_order`: each wavenumber 0 to 511 stands at exactly one slot.
All inputs are finite; a program needn't handle non-finite values.
Results may differ from a plain program's by a relative error of at most 0.0077.
Values may be sent and summed in bfloat16 or wider, within the bound.
A program may use at most 128 MiB of HBM per device.

v0:
```python
import functools
import math

import jax
import jax.numpy as jnp
from jax import lax
from jax.experimental import pallas as pl
from jax.experimental.pallas import tpu as pltpu
from jax.sharding import PartitionSpec as P

BLK = 64
MESH = pl.DeviceIdType.MESH

X, ZHI, CORE, ZLO, Y = 4, 4, 2, 4, 4
PLANE = X * CORE * Y
SIDES, DESTS = 2, 8
GROUP_STEP = ((3, 3, 3, 3, 2, 2, 0, 0), (1, 1, 1, 1, 2, 2, 0, 0))
GROUP_PLACE = ((0, 1, 2, 3, 2, 3, 0, 1), (0, 1, 2, 3, 0, 1, 2, 3))
ROWS = 2
AHEAD = 4


def place():
    lat, lon = lax.axis_index("lat"), lax.axis_index("lon")
    return lat // (ZHI * CORE), lat // CORE % ZHI, lat % CORE, lon // Y, lon % Y


def device(x, hi, core, lo, y):
    return ((x * ZHI + hi) * CORE + core, lo * Y + y)


def zonal_kernel(
    rows, share, steps,
    grid_ref, u_ref, v_ref, cos_ref, sin_ref, out_ref,
    grid, basis, right_in, left_in, right_out, left_out, packed, total,
    grid_sem, grid_send, right_send, right_recv, left_send, left_recv,
    pack_send, out_sem,
):
    x, hi, core, lo, y = place()
    lat_local, lon_local = grid_ref.shape[1:]
    half = basis.shape[1] // 2
    width = half // DESTS

    barrier = pltpu.get_barrier_semaphore()
    for step in range(1, Y):
        pl.semaphore_signal(
            barrier, inc=1, device_id=device(x, hi, core, lo, (y + step) % Y), device_id_type=MESH
        )
    for step in range(1, ZHI * ZLO):
        z = (hi * ZLO + lo + step) % (ZHI * ZLO)
        pl.semaphore_signal(
            barrier, inc=1, device_id=device(x, z // ZLO, core, z % ZLO, y), device_id_type=MESH
        )
    pl.semaphore_wait(barrier, Y - 1 + ZHI * ZLO - 1)

    def first_row(owner):
        return jnp.minimum(owner * share, rows - share)

    def grid_copies(step):
        columns = pl.ds(pl.multiple_of(y * lon_local, lon_local), lon_local)
        target = grid.at[pl.ds(step * ROWS, ROWS), :, columns]
        for offset in range(1, Y):
            owner = (y + offset) % Y
            pltpu.make_async_remote_copy(
                src_ref=grid_ref.at[pl.ds(first_row(owner) + step * ROWS, ROWS)],
                dst_ref=target,
                send_sem=grid_send,
                recv_sem=grid_sem.at[step],
                device_id=device(x, hi, core, lo, owner),
                device_id_type=MESH,
            ).start()
        pltpu.make_async_copy(
            grid_ref.at[pl.ds(first_row(y) + step * ROWS, ROWS)], target, grid_sem.at[step]
        ).start()

    for step in range(AHEAD):
        grid_copies(step)

    coarse, fine = u_ref.shape[0], cos_ref.shape[0]

    def fill(a, carry):
        piece = u_ref[pl.ds(a, 1), :] * cos_ref[...] + v_ref[pl.ds(a, 1), :] * sin_ref[...]
        basis[pl.ds(pl.multiple_of(a * fine, fine), fine), :] = piece.astype(basis.dtype)
        return carry

    lax.fori_loop(0, coarse, fill, 0)

    def product(step, side):
        left = grid[pl.ds(step * ROWS, ROWS)].reshape(ROWS * lat_local, grid.shape[2])
        return jnp.dot(
            left, basis[:, side * half : (side + 1) * half], preferred_element_type=jnp.float32
        )

    def hand_out(step, side):
        for pair in range(DESTS // 2):
            lanes = slice(pair * 2 * width, (pair + 1) * 2 * width)
            top, low = total[:lat_local, lanes], total[lat_local:, lanes]
            for odd in range(2):
                part = slice(odd * width, (odd + 1) * width)
                packed[step, pair * 2 + odd] = jnp.concatenate(
                    [top[:, part], low[:, part]], axis=1
                ).astype(packed.dtype)
        own_lo = ZLO - 1 if side else 0
        for dest in range(DESTS):
            to_hi = (hi + GROUP_STEP[side][dest]) % ZHI
            to_lo = GROUP_PLACE[side][dest]
            if GROUP_STEP[side][dest] == 0 and to_lo == own_lo:
                pltpu.make_async_copy(packed.at[step, dest], out_ref.at[step, hi], out_sem).start()
            else:
                pltpu.make_async_remote_copy(
                    src_ref=packed.at[step, dest],
                    dst_ref=out_ref.at[step, hi],
                    send_sem=pack_send,
                    recv_sem=out_sem,
                    device_id=device(x, to_hi, core, to_lo, y),
                    device_id_type=MESH,
                ).start()

    def chain(step, side):
        arrived, leaving = (right_in, right_out) if side else (left_in, left_out)
        send_sem, recv_sem = (right_send, right_recv) if side else (left_send, left_recv)
        first, last = (0, ZLO - 1) if side else (ZLO - 1, 0)
        total[...] = product(step, side)

        @pl.when(lo != first)
        def _():
            pltpu.make_async_copy(arrived.at[step], arrived.at[step], recv_sem.at[step]).wait()
            total[...] += arrived[step].astype(jnp.float32)

        @pl.when(lo != last)
        def _():
            leaving[step] = total[...].astype(leaving.dtype)
            pltpu.make_async_remote_copy(
                src_ref=leaving.at[step],
                dst_ref=arrived.at[step],
                send_sem=send_sem,
                recv_sem=recv_sem.at[step],
                device_id=device(x, hi, core, lo + (1 if side else -1), y),
                device_id_type=MESH,
            ).start()

        @pl.when(lo == last)
        def _():
            hand_out(step, side)

    def one(step, carry):
        @pl.when(step + AHEAD < steps)
        def _():
            grid_copies(step + AHEAD)

        first = step - jnp.minimum(lo, ZLO - 1 - lo)

        @pl.when((first >= 0) & (first < steps))
        def _():
            block = grid.at[pl.ds(first * ROWS, ROWS)]
            pltpu.make_async_copy(block, block, grid_sem.at[first]).wait()

        for side in range(SIDES):
            at = step - (lo if side else ZLO - 1 - lo)

            @pl.when((at >= 0) & (at < steps))
            def _():
                chain(at, side)

        return carry

    lax.fori_loop(0, steps + ZLO - 1, one, 0)

    sent = grid_ref.at[pl.ds(0, (Y - 1) * share)]
    pltpu.make_async_copy(sent, sent, grid_send).wait()

    @pl.when(lo != ZLO - 1)
    def _():
        pltpu.make_async_copy(right_out, right_out, right_send).wait()

    @pl.when(lo != 0)
    def _():
        pltpu.make_async_copy(left_out, left_out, left_send).wait()

    @pl.when((lo == 0) | (lo == ZLO - 1))
    def _():
        sent = packed.at[:, pl.ds(0, DESTS - 1)]
        pltpu.make_async_copy(sent, sent, pack_send).wait()

    pltpu.make_async_copy(out_ref, out_ref, out_sem).wait()


def zonal_sums(grid, waves):
    _, _, _, lo, _ = place()
    rows, lat_local, lon_local = grid.shape
    lon = lon_local * Y
    share = -(-rows // (Y * ROWS)) * ROWS
    steps = share // ROWS
    columns = 2 * waves.size
    fine = 32
    waves = jnp.broadcast_to(waves[:, :, None, :], waves.shape[:2] + (2, PLANE))
    sine = jnp.broadcast_to(jnp.arange(2)[None, None, :, None], waves.shape).reshape(1, columns) == 1
    waves = waves.reshape(1, columns)
    grid_lon = lon * ZLO

    def angles(longitudes):
        phases = longitudes[:, None] * waves % grid_lon
        return 2.0 * math.pi / grid_lon * phases.astype(jnp.float32)

    base = angles(lo * lon + fine * jnp.arange(lon // fine, dtype=jnp.int32))
    near = angles(jnp.arange(fine, dtype=jnp.int32))
    scale = math.sqrt(2.0 / grid_lon)
    base_cos, base_sin = jnp.cos(base) * scale, jnp.sin(base) * scale
    u = jnp.where(sine, base_sin, base_cos)
    v = jnp.where(sine, base_cos, -base_sin)
    half = columns // 2
    packed = (lat_local, ROWS * half // DESTS)
    chain = pltpu.VMEM((steps, ROWS * lat_local, half), jnp.bfloat16)
    vmem = pl.BlockSpec(memory_space=pltpu.VMEM)
    hbm = pl.BlockSpec(memory_space=pl.ANY)
    dma = pltpu.SemaphoreType.DMA
    return pl.pallas_call(
        functools.partial(zonal_kernel, rows, share, steps),
        out_shape=jax.ShapeDtypeStruct((steps, ZHI) + packed, jnp.bfloat16),
        in_specs=[hbm, vmem, vmem, vmem, vmem],
        out_specs=hbm,
        scratch_shapes=[
            pltpu.VMEM((share, lat_local, lon), jnp.bfloat16),
            pltpu.VMEM((lon, columns), jnp.bfloat16),
            chain,
            chain,
            chain,
            chain,
            pltpu.VMEM((steps, DESTS) + packed, jnp.bfloat16),
            pltpu.VMEM((ROWS * lat_local, half), jnp.float32),
            dma((steps,)),
            dma,
            dma,
            dma((steps,)),
            dma,
            dma((steps,)),
            dma,
            dma,
        ],
        compiler_params=pltpu.CompilerParams(
            collective_id=0, has_side_effects=True, vmem_limit_bytes=48 << 20
        ),
    )(grid, u, v, jnp.cos(near), jnp.sin(near))


def plane_kernel(in_ref, out_ref, send_sem, recv_sem):
    x, hi, core, lo, y = place()
    mine = (x * CORE + core) * Y + y

    def peer(offset):
        other = (mine + offset) % PLANE
        return other, device(other // (CORE * Y), hi, other // Y % CORE, lo, other % Y)

    barrier = pltpu.get_barrier_semaphore()

    def greet(offset, carry):
        pl.semaphore_signal(barrier, inc=1, device_id=peer(offset)[1], device_id_type=MESH)
        return carry

    lax.fori_loop(1, PLANE, greet, 0)
    pl.semaphore_wait(barrier, PLANE - 1)
    pltpu.make_async_copy(in_ref.at[mine], out_ref.at[mine], recv_sem).start()

    def send(offset, carry):
        other, where = peer(offset)
        pltpu.make_async_remote_copy(
            src_ref=in_ref.at[other],
            dst_ref=out_ref.at[mine],
            send_sem=send_sem,
            recv_sem=recv_sem,
            device_id=where,
            device_id_type=MESH,
        ).start()
        return carry

    lax.fori_loop(1, PLANE, send, 0)
    sent = in_ref.at[pl.ds(0, PLANE - 1)]
    pltpu.make_async_copy(sent, sent, send_sem).wait()
    pltpu.make_async_copy(out_ref, out_ref, recv_sem).wait()


def plane_exchange(blocks):
    hbm = pl.BlockSpec(memory_space=pl.ANY)
    return pl.pallas_call(
        plane_kernel,
        out_shape=jax.ShapeDtypeStruct(blocks.shape, blocks.dtype),
        in_specs=[hbm],
        out_specs=hbm,
        scratch_shapes=[pltpu.SemaphoreType.DMA, pltpu.SemaphoreType.DMA],
        compiler_params=pltpu.CompilerParams(collective_id=1, has_side_effects=True),
    )(blocks)


def meridional_table(grid_lat, lat_local):
    modes = jnp.arange(grid_lat, dtype=jnp.int32)
    owner = jnp.arange(X * ZHI * CORE, dtype=jnp.int32).reshape(X, ZHI, CORE)
    owner = owner.transpose(0, 2, 1).reshape(-1)

    def angles(halves):
        phases = modes[None, :] * halves[:, None] % (4 * grid_lat)
        return math.pi / (2 * grid_lat) * phases.astype(jnp.float32)

    base = angles(2 * lat_local * owner)
    near = angles(2 * jnp.arange(lat_local, dtype=jnp.int32) + 1)
    scale = math.sqrt(2.0 / grid_lat)
    base_cos, base_sin = jnp.cos(base)[:, None] * scale, jnp.sin(base)[:, None] * scale
    table = base_cos * jnp.cos(near)[None] - base_sin * jnp.sin(near)[None]
    return table.reshape(grid_lat, grid_lat).astype(jnp.bfloat16)


def band_apply(blocks, diagonal_blocks, lower_blocks):
    result = jnp.einsum(
        "bij,crbj->crbi", diagonal_blocks, blocks, preferred_element_type=jnp.float32
    )
    below = jnp.einsum(
        "bij,crbj->crbi", lower_blocks, blocks[:, :, :-1], preferred_element_type=jnp.float32
    )
    above = jnp.einsum(
        "bji,crbj->crbi", lower_blocks, blocks[:, :, 1:], preferred_element_type=jnp.float32
    )
    below = jnp.pad(below, ((0, 0), (0, 0), (1, 0), (0, 0)))
    above = jnp.pad(above, ((0, 0), (0, 0), (0, 1), (0, 0)))
    return result + below + above


def per_device(cotangent, wave_order, band_diagonal, band_lower, vertical_matrix):
    fields, levels, lat_local, lon_local = cotangent.shape
    rows = fields * levels
    grid_lat = lat_local * X * ZHI * CORE
    _, hi, _, _, _ = place()
    to_hi = (hi + jnp.array(GROUP_STEP)) % ZHI
    plane = jnp.arange(PLANE)
    slots = (to_hi * CORE * ZLO + jnp.array(GROUP_PLACE))[:, :, None] * Y + (
        (plane // (CORE * Y) * ZHI * CORE + plane // Y % CORE) * ZLO * Y + plane % Y
    )
    coeffs = zonal_sums(cotangent.reshape(rows, lat_local, lon_local), wave_order[slots])
    steps = coeffs.shape[0]
    share = steps * ROWS
    coeffs = coeffs.reshape(steps, ZHI, lat_local, ROWS, 2, PLANE)
    blocks = coeffs.transpose(5, 4, 0, 3, 1, 2).reshape(PLANE, -1, 128)
    gathered = plane_exchange(blocks).reshape(X * CORE, Y, 2, share, ZHI * lat_local)
    gathered = gathered.transpose(2, 1, 3, 0, 4).reshape(2, Y * share, grid_lat)
    spare = Y * share - rows
    gathered = jnp.concatenate(
        [gathered[:, : (Y - 1) * share], gathered[:, (Y - 1) * share + spare :]], axis=1
    )
    spectra = jnp.einsum(
        "crn,nk->crk",
        gathered,
        meridional_table(grid_lat, lat_local),
        preferred_element_type=jnp.float32,
    ).astype(jnp.bfloat16)
    block_count = band_diagonal.shape[1]
    diagonal_blocks = band_diagonal[0].reshape(block_count, BLK, BLK)
    lower_blocks = band_lower[0].reshape(block_count - 1, BLK, BLK)
    blocks = spectra.reshape(2, rows, block_count, BLK)
    banded = band_apply(blocks, diagonal_blocks, lower_blocks).astype(jnp.bfloat16)
    layered = banded.reshape(2, fields, levels, grid_lat)
    mixed = jnp.einsum(
        "flm,cflk->cfmk", vertical_matrix, layered, preferred_element_type=jnp.float32
    )
    return mixed.astype(jnp.bfloat16)[None]


def solution(mesh):
    return jax.shard_map(
        per_device,
        mesh=mesh,
        in_specs=(
            P(None, None, "lat", "lon"),
            P(),
            P(("lat", "lon"), None, None),
            P(("lat", "lon"), None, None),
            P(),
        ),
        out_specs=P(("lat", "lon"), None, None, None, None),
        check_vma=False,
    )
```

profile of v0, /device:TPU:1, one launch (start us, length us, event | category | flops | bytes accessed | tf_op | source)
XLA Modules:
  0.0 186.0 jit_solution(14910752600692781599)
XLA Ops:
  0.0 0.7 fusion.38
  1.0 3.5 %gather_fusion = s32[512]{0:T(512)S(1)} fusion(s32[512]{0:T(512)S(1)} %copy-done.2, s32[1024]{0:T(1024)S(1)} %pad_clamp_fusion), kind=kCustom, calls=%fused_computation | custom fusion | bytes 6144 | tf_op jit(solution)/shard_map/gather | solution.py:336
  4.8 1.1 reshape.262
  5.9 1.1 reshape_squeeze.7
  7.0 1.6 cosine_multiply_fusion
  8.7 1.1 reshape.261
  9.8 1.1 negate_select_fusion.3
  10.9 2.0 %copy-done.1 = bf16[3,50,48,256]{3,2,1,0:T(8,128)(2,1)S(1)} copy-done((bf16[3,50,48,256]{3,2,1,0:T(8,128)(2,1)S(1)}, bf16[3,50,48,256]{3,2,1,0:T(8,128)(2,1)}, u32[]{:S(2)}) %copy-start.1) | copy-done | bytes 3686424
  12.9 107.1 %shard_map.73 = bf16[19,4,48,128]{3,2,1,0:T(8,128)(2,1)S(1)} custom-call(bf16[150,48,256]{2,1,0:T(8,128)(2,1)S(1)} %bitcast.52, f32[32,1024]{1,0:T(8,128)S(1)} %get-tuple-element.6.u_ref, f32[32,1024]{1,0:T(8,128)S(1)} %get-tuple-element.5.v_ref, f32[32,1024]{1,0:T(8,128)S(1)} %get-tuple-element.8.cos_ref, f32[32,1024]{1,0:T(8,128)S(1)} %get-tuple-element.7.sin_ref), custom_call_target="tpu_custom_call" | custom-call | tf_op jit(solution)/shard_map/pallas_call | solution.py:217
  120.0 2.1 %fusion.15 = (f32[48,1536]{1,0:T(8,128)}, f32[48,1536]{1,0:T(8,128)}) fusion(s32[48]{0:T(128)S(1)} %multiply_add_fusion), kind=kLoop, calls=%fused_computation.25 | loop fusion | flops 663552 | bytes 590016 | tf_op jit(solution)/shard_map/cos | solution.py:307
  122.1 2.4 %copy.16 = bf16[19,4,48,128]{2,3,1,0:T(8,128)(2,1)S(1)} copy(bf16[19,4,48,128]{3,2,1,0:T(8,128)(2,1)S(1)} %shard_map.73) | data formatting | bytes 1867776 | tf_op jit(solution)/shard_map/pallas_call | solution.py:217
  124.5 3.4 %copy.17 = bf16[32,2,19,2,4,48]{5,4,3,2,1,0:T(4,128)(2,1)} copy(bf16[32,2,19,2,4,48]{5,0,1,3,4,2:T(8,128)(2,1)S(1)} %bitcast.53) | data formatting | bytes 1867776 | tf_op jit(solution)/shard_map/transpose | solution.py:340
  127.9 6.3 %reshape.242.in_ref = bf16[32,114,128]{2,1,0:T(8,128)(2,1)} reshape(bf16[32,2,19,2,4,48]{5,4,3,2,1,0:T(4,128)(2,1)} %copy.17) | data formatting | bytes 1867776 | tf_op jit(solution)/shard_map/reshape | solution.py:340
  134.3 32.0 %shard_map.74 = bf16[32,114,128]{2,1,0:T(8,128)(2,1)} custom-call(bf16[32,114,128]{2,1,0:T(8,128)(2,1)} %reshape.242.in_ref), custom_call_target="tpu_custom_call" | custom-call | tf_op jit(solution)/shard_map/pallas_call | solution.py:284
  166.3 2.7 %reshape.243 = bf16[8,4,2,38,192]{4,3,2,1,0:T(8,128)(2,1)S(1)} reshape(bf16[32,114,128]{2,1,0:T(8,128)(2,1)} %shard_map.74) | data formatting | bytes 1867776 | tf_op jit(solution)/shard_map/reshape | solution.py:341
  169.7 1.3 reshape.244
  171.1 1.8 subtract_convert_fusion
  173.0 1.6 convolution_convert_fusion.1
  174.6 1.1 reshape.249
  175.7 1.6 copy.19
  177.4 1.6 convolution_bitcast_fusion
  180.6 2.1 %copy.23 = bf16[2,150,24,64]{3,2,0,1:T(8,128)(2,1)S(1)} copy(bf16[2,150,24,64]{1,3,0,2:T(8,128)(2,1)S(1)} %fusion.1) | data formatting | bytes 1843200 | tf_op jit(solution)/shard_map/convert_element_type | solution.py:357
  182.7 1.2 reshape.250
  184.4 1.6 copy.26
  (40 shorter events, 3.4 us)
Async XLA Ops:
  0.0 183.9 %copy-start = (bf16[3,50,50]{2,1,0:T(8,128)(2,1)S(1)}, bf16[3,50,50]{2,1,0:T(8,128)(2,1)}, u32[]{:S(2)}) copy-start(bf16[3,50,50]{2,1,0:T(8,128)(2,1)} %param.11) | copy-start | bytes 45004
  0.0 1.0 copy-start.2
  1.0 3.8 %copy-start.9 = (bf16[1,23,4096]{2,1,0:T(8,128)(2,1)S(1)}, bf16[1,23,4096]{2,1,0:T(8,128)(2,1)}, u32[]{:S(2)}) copy-start(bf16[1,23,4096]{2,1,0:T(8,128)(2,1)} %param.10) | copy-start | bytes 565252
  1.0 7.6 %copy-start.10 = (bf16[1,24,4096]{2,1,0:T(8,128)(2,1)S(1)}, bf16[1,24,4096]{2,1,0:T(8,128)(2,1)}, u32[]{:S(2)}) copy-start(bf16[1,24,4096]{2,1,0:T(8,128)(2,1)} %param.9) | copy-start | bytes 589828
  10.9 2.0 %copy-start.1 = (bf16[3,50,48,256]{3,2,1,0:T(8,128)(2,1)S(1)}, bf16[3,50,48,256]{3,2,1,0:T(8,128)(2,1)}, u32[]{:S(2)}) copy-start(bf16[3,50,48,256]{3,2,1,0:T(8,128)(2,1)} %param.7) | copy-start | bytes 11059204
  169.0 2.1 %copy-start.5 = (f32[48,1536]{1,0:T(8,128)S(1)}, f32[48,1536]{1,0:T(8,128)}, u32[]{:S(2)}) copy-start(f32[48,1536]{1,0:T(8,128)} %get-tuple-element.11) | copy-start | bytes 884740
  169.0 2.1 %copy-start.6 = (f32[48,1536]{1,0:T(8,128)S(1)}, f32[48,1536]{1,0:T(8,128)}, u32[]{:S(2)}) copy-start(f32[48,1536]{1,0:T(8,128)} %get-tuple-element.12) | copy-start | bytes 884740
  169.0 2.1 %copy-start.7 = (f32[32,1536]{1,0:T(8,128)S(1)}, f32[32,1536]{1,0:T(8,128)}, u32[]{:S(2)}) copy-start(f32[32,1536]{1,0:T(8,128)} %get-tuple-element.9) | copy-start | bytes 589828
  169.7 1.4 copy-start.8
  177.4 1.6 copy-start.4
  179.0 1.0 copy-start.3
where the time goes:
time: 186 us
  Pallas kernels  139 us (75%)
  local copies, waits for them, and re-layouts  34.3 us (18%)
  other arithmetic  7.47 us (4%)
  matrix products  4.84 us (3%)
    pallas_call x1, Pallas kernels, zonal_sums(): pl.pallas_call(functools.partial(zonal_kernel, rows, share, steps), out_s...  107 us
    pallas_call x1, Pallas kernels, plane_exchange(): pl.pallas_call(plane_kernel, out_shape=jax.ShapeDtypeStruct(blocks.shape,...  32 us
    reshape x1, local copies, waits for them, and re-layouts, per_device(): blocks = coeffs.transpose(5, 4, 0, 3, 1, 2).reshape(PLANE, -1, 128)  6.34 us

commit v1 on v0

--- a/solution.py
+++ b/solution.py
@@ -18,6 +18,8 @@
 GROUP_PLACE = ((0, 1, 2, 3, 2, 3, 0, 1), (0, 1, 2, 3, 0, 1, 2, 3))
 ROWS = 2
 AHEAD = 4
+COARSE = 32
+SKEW = 2
 
 
 def place():
@@ -29,10 +31,52 @@
     return ((x * ZHI + hi) * CORE + core, lo * Y + y)
 
 
+def cosine(phase, period):
+    quarter = period // 4
+    turns = jnp.floor(phase * (1.0 / quarter) + 0.5)
+    angle = (phase - turns * quarter) * (2.0 * math.pi / period)
+    square = angle * angle
+    even = 1.0 + square * (
+        -1 / 2 + square * (1 / 24 + square * (-1 / 720 + square * (1 / 40320)))
+    )
+    odd = angle * (
+        1.0 + square * (-1 / 6 + square * (1 / 120 + square * (-1 / 5040 + square * (1 / 362880))))
+    )
+    turn = turns.astype(jnp.int32) & 3
+    value = jnp.where((turn & 1) == 1, odd, even)
+    return jnp.where((turn == 1) | (turn == 2), -value, value)
+
+
+def slots_of_columns(hi, column):
+    width = 2 * PLANE
+    side, dest, plane = column // (DESTS * width), column // width % DESTS, column % PLANE
+    step = jnp.where(dest < 4, jnp.where(side == 0, 3, 1), jnp.where(dest < 6, 2, 0))
+    low_side = jnp.where(dest < 4, dest, jnp.where(dest < 6, dest - 2, dest - 6))
+    lo = jnp.where(side == 0, low_side, dest % 4)
+    lo = jnp.where((side == 1) & (dest >= 6), dest - 4, lo)
+    to_hi = (hi + step) % ZHI
+    x, core, y = plane // (CORE * Y), plane // Y % CORE, plane % Y
+    return (((x * ZHI + to_hi) * CORE + core) * ZLO + lo) * Y + y
+
+
+def waves_of_columns(wave_ref, hi, columns):
+    slots = wave_ref.shape[1]
+    slot = slots_of_columns(hi, lax.broadcasted_iota(jnp.int32, (1, columns), 1))
+    wave = jnp.broadcast_to(wave_ref[...], (8, slots))
+    pick = lax.broadcasted_iota(jnp.int32, (slots, columns), 0) == slot
+    pick = jnp.where(pick, 1.0, 0.0).astype(jnp.bfloat16)
+
+    def picked(digits):
+        digits = digits.astype(jnp.float32).astype(jnp.bfloat16)
+        return jnp.dot(digits, pick, preferred_element_type=jnp.float32)[:1]
+
+    return picked(wave // 16) * 16.0 + picked(wave % 16)
+
+
 def zonal_kernel(
     rows, share, steps,
-    grid_ref, u_ref, v_ref, cos_ref, sin_ref, out_ref,
-    grid, basis, right_in, left_in, right_out, left_out, packed, total,
+    grid_ref, wave_ref, out_ref,
+    grid, basis, u_ref, v_ref, right_in, left_in, right_out, left_out, packed, total,
     grid_sem, grid_send, right_send, right_recv, left_send, left_recv,
     pack_send, out_sem,
 ):
@@ -76,10 +120,21 @@
     for step in range(AHEAD):
         grid_copies(step)
 
-    coarse, fine = u_ref.shape[0], cos_ref.shape[0]
+    waves = waves_of_columns(wave_ref, hi, basis.shape[1])
+    column = lax.broadcasted_iota(jnp.int32, (1, basis.shape[1]), 1)
+    sine = jnp.where(column // PLANE % 2 == 1, 1.0, 0.0)
+    lon, grid_lon = basis.shape[0], basis.shape[0] * ZLO
+    coarse, fine = u_ref.shape[0], lon // u_ref.shape[0]
+    scale = math.sqrt(2.0 / grid_lon)
+    first = (lo * lon + fine * lax.broadcasted_iota(jnp.int32, (coarse, 1), 0)).astype(jnp.float32)
+    base = waves * first - sine * (grid_lon // 4)
+    u_ref[...] = cosine(base, grid_lon) * scale
+    v_ref[...] = cosine(base + grid_lon // 4, grid_lon) * scale
+    near = waves * lax.broadcasted_iota(jnp.int32, (fine, 1), 0).astype(jnp.float32)
+    near_cos, near_sin = cosine(near, grid_lon), cosine(near - grid_lon // 4, grid_lon)
 
     def fill(a, carry):
-        piece = u_ref[pl.ds(a, 1), :] * cos_ref[...] + v_ref[pl.ds(a, 1), :] * sin_ref[...]
+        piece = u_ref[pl.ds(a, 1), :] * near_cos + v_ref[pl.ds(a, 1), :] * near_sin
         basis[pl.ds(pl.multiple_of(a * fine, fine), fine), :] = piece.astype(basis.dtype)
         return carry
 
@@ -148,7 +203,7 @@
         def _():
             grid_copies(step + AHEAD)
 
-        first = step - jnp.minimum(lo, ZLO - 1 - lo)
+        first = step - SKEW * jnp.minimum(lo, ZLO - 1 - lo)
 
         @pl.when((first >= 0) & (first < steps))
         def _():
@@ -156,7 +211,7 @@
             pltpu.make_async_copy(block, block, grid_sem.at[first]).wait()
 
         for side in range(SIDES):
-            at = step - (lo if side else ZLO - 1 - lo)
+            at = step - SKEW * (lo if side else ZLO - 1 - lo)
 
             @pl.when((at >= 0) & (at < steps))
             def _():
@@ -164,7 +219,7 @@
 
         return carry
 
-    lax.fori_loop(0, steps + ZLO - 1, one, 0)
+    lax.fori_loop(0, steps + SKEW * (ZLO - 1), one, 0)
 
     sent = grid_ref.at[pl.ds(0, (Y - 1) * share)]
     pltpu.make_async_copy(sent, sent, grid_send).wait()
@@ -185,43 +240,27 @@
     pltpu.make_async_copy(out_ref, out_ref, out_sem).wait()
 
 
-def zonal_sums(grid, waves):
-    _, _, _, lo, _ = place()
+def zonal_sums(grid, wave_order):
     rows, lat_local, lon_local = grid.shape
     lon = lon_local * Y
     share = -(-rows // (Y * ROWS)) * ROWS
     steps = share // ROWS
-    columns = 2 * waves.size
-    fine = 32
-    waves = jnp.broadcast_to(waves[:, :, None, :], waves.shape[:2] + (2, PLANE))
-    sine = jnp.broadcast_to(jnp.arange(2)[None, None, :, None], waves.shape).reshape(1, columns) == 1
-    waves = waves.reshape(1, columns)
-    grid_lon = lon * ZLO
-
-    def angles(longitudes):
-        phases = longitudes[:, None] * waves % grid_lon
-        return 2.0 * math.pi / grid_lon * phases.astype(jnp.float32)
-
-    base = angles(lo * lon + fine * jnp.arange(lon // fine, dtype=jnp.int32))
-    near = angles(jnp.arange(fine, dtype=jnp.int32))
-    scale = math.sqrt(2.0 / grid_lon)
-    base_cos, base_sin = jnp.cos(base) * scale, jnp.sin(base) * scale
-    u = jnp.where(sine, base_sin, base_cos)
-    v = jnp.where(sine, base_cos, -base_sin)
+    columns = 2 * wave_order.size
     half = columns // 2
     packed = (lat_local, ROWS * half // DESTS)
     chain = pltpu.VMEM((steps, ROWS * lat_local, half), jnp.bfloat16)
-    vmem = pl.BlockSpec(memory_space=pltpu.VMEM)
     hbm = pl.BlockSpec(memory_space=pl.ANY)
     dma = pltpu.SemaphoreType.DMA
     return pl.pallas_call(
         functools.partial(zonal_kernel, rows, share, steps),
         out_shape=jax.ShapeDtypeStruct((steps, ZHI) + packed, jnp.bfloat16),
-        in_specs=[hbm, vmem, vmem, vmem, vmem],
+        in_specs=[hbm, pl.BlockSpec(memory_space=pltpu.VMEM)],
         out_specs=hbm,
         scratch_shapes=[
             pltpu.VMEM((share, lat_local, lon), jnp.bfloat16),
             pltpu.VMEM((lon, columns), jnp.bfloat16),
+            pltpu.VMEM((COARSE, columns), jnp.float32),
+            pltpu.VMEM((COARSE, columns), jnp.float32),
             chain,
             chain,
             chain,
@@ -238,14 +277,27 @@
             dma,
         ],
         compiler_params=pltpu.CompilerParams(
-            collective_id=0, has_side_effects=True, vmem_limit_bytes=48 << 20
+            collective_id=0, has_side_effects=True, vmem_limit_bytes=61 << 20
         ),
-    )(grid, u, v, jnp.cos(near), jnp.sin(near))
-
-
-def plane_kernel(in_ref, out_ref, send_sem, recv_sem):
+    )(grid, wave_order.reshape(1, -1))
+
+
+def mode_kernel(
+    rows, share,
+    in_ref, diagonal_ref, lower_ref, vertical_ref, out_ref,
+    wide, spread, sending, gathered, table, base_cos, base_sin,
+    diagonal, lower, band, levels_pad, mix, spectra, banded, total,
+    send_sem, recv_sem,
+):
     x, hi, core, lo, y = place()
     mine = (x * CORE + core) * Y + y
+    steps, _, lat_local, _ = in_ref.shape
+    span = ZHI * lat_local
+    depth = sending.shape[1]
+    fields, levels = vertical_ref.shape[:2]
+    grid_lat = table.shape[1]
+    blocks = diagonal_ref.shape[0]
+    f32, bf16 = jnp.float32, jnp.bfloat16
 
     def peer(offset):
         other = (mine + offset) % PLANE
@@ -258,14 +310,39 @@
         return carry
 
     lax.fori_loop(1, PLANE, greet, 0)
+
+    wide[...] = jnp.zeros_like(wide)
+    for row in range(4 * steps, depth):
+        for part in range(2):
+            spread[part, pl.ds(row, PLANE, stride=depth), :] = jnp.zeros((PLANE, 128), f32)
+
+    def turn(step, carry):
+        wide[:span, :] = in_ref[step].reshape(span, 128).astype(f32)
+        turned = wide[...].T
+        for group in range(4):
+            for part in range(2):
+                spread[part, pl.ds(4 * step + group, PLANE, stride=depth), :] = turned[
+                    group * PLANE : (group + 1) * PLANE, part * 128 : (part + 1) * 128
+                ]
+        return carry
+
+    lax.fori_loop(0, steps, turn, 0)
+
+    def narrow(other, carry):
+        at = pl.ds(pl.multiple_of(other * depth, depth), depth)
+        for part in range(2):
+            sending[other, :, part * 128 : (part + 1) * 128] = spread[part, at, :].astype(bf16)
+        return carry
+
+    lax.fori_loop(0, PLANE, narrow, 0)
+
     pl.semaphore_wait(barrier, PLANE - 1)
-    pltpu.make_async_copy(in_ref.at[mine], out_ref.at[mine], recv_sem).start()
 
     def send(offset, carry):
         other, where = peer(offset)
         pltpu.make_async_remote_copy(
-            src_ref=in_ref.at[other],
-            dst_ref=out_ref.at[mine],
+            src_ref=sending.at[other],
+            dst_ref=gathered.at[mine],
             send_sem=send_sem,
             recv_sem=recv_sem,
             device_id=where,
@@ -274,92 +351,153 @@
         return carry
 
     lax.fori_loop(1, PLANE, send, 0)
-    sent = in_ref.at[pl.ds(0, PLANE - 1)]
+    pltpu.make_async_copy(sending.at[mine], gathered.at[mine], recv_sem).start()
+
+    scale = math.sqrt(2.0 / grid_lat)
+    mode = lax.broadcasted_iota(jnp.int32, (1, grid_lat), 1).astype(f32)
+    owners = X * ZHI * CORE
+    base = 2 * lat_local * lax.broadcasted_iota(jnp.int32, (owners, 1), 0)
+    base = base.astype(f32) * mode
+    base_cos[...] = cosine(base, 4 * grid_lat) * scale
+    base_sin[...] = cosine(base - grid_lat, 4 * grid_lat) * scale
+    near = (2 * lax.broadcasted_iota(jnp.int32, (lat_local, 1), 0) + 1).astype(f32) * mode
+    near_cos, near_sin = cosine(near, 4 * grid_lat), cosine(near - grid_lat, 4 * grid_lat)
+
+    def fill(owner, carry):
+        to_x, to_hi, to_core = owner // (ZHI * CORE), owner // CORE % ZHI, owner % CORE
+        at = (to_x * CORE + to_core) * 256 + to_hi * lat_local
+        piece = base_cos[pl.ds(owner, 1), :] * near_cos - base_sin[pl.ds(owner, 1), :] * near_sin
+        table[pl.ds(pl.multiple_of(at, 16), lat_local), :] = piece.astype(bf16)
+        return carry
+
+    lax.fori_loop(0, owners, fill, 0)
+    for source in range(X * CORE):
+        table[source * 256 + span : (source + 1) * 256, :] = jnp.zeros((256 - span, grid_lat), bf16)
+
+    for row in range(BLK):
+        tile = slice(row // 2 * 128, row // 2 * 128 + 128)
+        for flat, square in ((diagonal_ref, diagonal), (lower_ref, lower)):
+            piece = flat[:, tile].astype(f32)
+            if row % 2:
+                piece = pltpu.roll(piece, 64, 1)
+            square[pl.ds(row, flat.shape[0], stride=BLK), :] = piece
+
+    empty = jnp.zeros((BLK, BLK), f32)
+
+    def square(ref, block):
+        return ref[block * BLK : (block + 1) * BLK, :BLK]
+
+    for pair in range(blocks // 2):
+        one, two = 2 * pair, 2 * pair + 1
+        before = square(lower, one - 1) if pair else empty
+        after = square(lower, two).T if two < blocks - 1 else empty
+        inner = square(lower, one)
+        top = (empty, before, square(diagonal, one), inner.T, empty, empty)
+        low = (empty, empty, inner, square(diagonal, two), after, empty)
+        band[pair, :BLK, :] = jnp.concatenate(top, axis=1).astype(bf16)
+        band[pair, BLK:, :] = jnp.concatenate(low, axis=1).astype(bf16)
+
+    held = mix.shape[1]
+    at = lax.broadcasted_iota(jnp.int32, (1, held), 1)
+    owner, within = at // depth, at % depth
+    start = jnp.minimum(owner * share, rows - share)
+    row = start + within // 2
+    fresh = (row >= owner * share) & (within < 2 * share)
+    level = lax.broadcasted_iota(jnp.int32, (BLK, 1), 0)
+    for field in range(fields):
+        levels_pad[...] = jnp.zeros_like(levels_pad)
+        levels_pad[:levels, :levels] = vertical_ref[field].astype(f32)
+        turned = levels_pad[...].T[:BLK, :].astype(bf16)
+        pick = (row == field * levels + level) & (level < levels) & fresh
+        pick = jnp.where(pick, 1.0, 0.0).astype(bf16)
+        pick = jnp.concatenate([pick, jnp.zeros((128 - BLK, held), bf16)], axis=0)
+        mixed = jnp.dot(turned, pick, preferred_element_type=f32)
+        for c in range(2):
+            part = c * fields + field
+            mix[part * BLK : (part + 1) * BLK, :] = jnp.where(at % 2 == c, mixed, 0.0).astype(bf16)
+
+    sent = sending.at[pl.ds(0, PLANE - 1)]
     pltpu.make_async_copy(sent, sent, send_sem).wait()
-    pltpu.make_async_copy(out_ref, out_ref, recv_sem).wait()
-
-
-def plane_exchange(blocks):
-    hbm = pl.BlockSpec(memory_space=pl.ANY)
+    pltpu.make_async_copy(gathered, gathered, recv_sem).wait()
+
+    width = total.shape[1]
+    for tile in range(grid_lat // width):
+        lanes = slice(tile * width, (tile + 1) * width)
+        for source in range(X * CORE):
+            left = gathered[source * Y : (source + 1) * Y].reshape(held, 256)
+            term = jnp.dot(
+                left, table[source * 256 : (source + 1) * 256, lanes], preferred_element_type=f32
+            )
+            if source == 0:
+                total[...] = term
+            else:
+                total[...] += term
+        spectra[:, lanes] = total[...].astype(bf16)
+
+    for pair in range(blocks // 2):
+        begin, end = max(0, pair - 1) * 128, min(blocks // 2, pair + 2) * 128
+        skip = 0 if pair else 128
+        banded[:, pair * 128 : (pair + 1) * 128] = lax.dot_general(
+            spectra[:, begin:end],
+            band[pair, :, skip : skip + end - begin],
+            (((1,), (1,)), ((), ())),
+            preferred_element_type=f32,
+        ).astype(bf16)
+
+    for tile in range(grid_lat // width):
+        lanes = slice(tile * width, (tile + 1) * width)
+        result = jnp.dot(mix[...], banded[:, lanes], preferred_element_type=f32)
+        for c in range(2):
+            for field in range(fields):
+                at = (c * fields + field) * BLK
+                out_ref[c, field, :, lanes] = result[at : at + levels].astype(out_ref.dtype)
+
+
+def finish(coeffs, diagonal, lower, vertical, rows, grid_lat):
+    fields, levels = vertical.shape[:2]
+    steps = coeffs.shape[0]
+    share = steps * ROWS
+    depth = -(-2 * share // 16) * 16
+    blocks = diagonal.shape[0]
+    vmem = pl.BlockSpec(memory_space=pltpu.VMEM)
+    f32, bf16 = jnp.float32, jnp.bfloat16
     return pl.pallas_call(
-        plane_kernel,
-        out_shape=jax.ShapeDtypeStruct(blocks.shape, blocks.dtype),
-        in_specs=[hbm],
-        out_specs=hbm,
-        scratch_shapes=[pltpu.SemaphoreType.DMA, pltpu.SemaphoreType.DMA],
-        compiler_params=pltpu.CompilerParams(collective_id=1, has_side_effects=True),
-    )(blocks)
-
-
-def meridional_table(grid_lat, lat_local):
-    modes = jnp.arange(grid_lat, dtype=jnp.int32)
-    owner = jnp.arange(X * ZHI * CORE, dtype=jnp.int32).reshape(X, ZHI, CORE)
-    owner = owner.transpose(0, 2, 1).reshape(-1)
-
-    def angles(halves):
-        phases = modes[None, :] * halves[:, None] % (4 * grid_lat)
-        return math.pi / (2 * grid_lat) * phases.astype(jnp.float32)
-
-    base = angles(2 * lat_local * owner)
-    near = angles(2 * jnp.arange(lat_local, dtype=jnp.int32) + 1)
-    scale = math.sqrt(2.0 / grid_lat)
-    base_cos, base_sin = jnp.cos(base)[:, None] * scale, jnp.sin(base)[:, None] * scale
-    table = base_cos * jnp.cos(near)[None] - base_sin * jnp.sin(near)[None]
-    return table.reshape(grid_lat, grid_lat).astype(jnp.bfloat16)
-
-
-def band_apply(blocks, diagonal_blocks, lower_blocks):
-    result = jnp.einsum(
-        "bij,crbj->crbi", diagonal_blocks, blocks, preferred_element_type=jnp.float32
-    )
-    below = jnp.einsum(
-        "bij,crbj->crbi", lower_blocks, blocks[:, :, :-1], preferred_element_type=jnp.float32
-    )
-    above = jnp.einsum(
-        "bji,crbj->crbi", lower_blocks, blocks[:, :, 1:], preferred_element_type=jnp.float32
-    )
-    below = jnp.pad(below, ((0, 0), (0, 0), (1, 0), (0, 0)))
-    above = jnp.pad(above, ((0, 0), (0, 0), (0, 1), (0, 0)))
-    return result + below + above
+        functools.partial(mode_kernel, rows, share),
+        out_shape=jax.ShapeDtypeStruct((2, fields, levels, grid_lat), bf16),
+        in_specs=[vmem] * 4,
+        out_specs=vmem,
+        scratch_shapes=[
+            pltpu.VMEM((256, 128), f32),
+            pltpu.VMEM((2, PLANE * depth, 128), f32),
+            pltpu.VMEM((PLANE, depth, 256), bf16),
+            pltpu.VMEM((PLANE, depth, 256), bf16),
+            pltpu.VMEM((X * CORE * 256, grid_lat), bf16),
+            pltpu.VMEM((X * ZHI * CORE, grid_lat), f32),
+            pltpu.VMEM((X * ZHI * CORE, grid_lat), f32),
+            pltpu.VMEM((blocks * BLK, 128), f32),
+            pltpu.VMEM(((blocks - 1) * BLK, 128), f32),
+            pltpu.VMEM((blocks // 2, 2 * BLK, 6 * BLK), bf16),
+            pltpu.VMEM((128, 128), f32),
+            pltpu.VMEM((2 * fields * BLK, Y * depth), bf16),
+            pltpu.VMEM((Y * depth, grid_lat), bf16),
+            pltpu.VMEM((Y * depth, grid_lat), bf16),
+            pltpu.VMEM((Y * depth, 512), f32),
+            pltpu.SemaphoreType.DMA,
+            pltpu.SemaphoreType.DMA,
+        ],
+        compiler_params=pltpu.CompilerParams(
+            collective_id=1, has_side_effects=True, vmem_limit_bytes=48 << 20
+        ),
+    )(coeffs, diagonal, lower, vertical)
 
 
 def per_device(cotangent, wave_order, band_diagonal, band_lower, vertical_matrix):
     fields, levels, lat_local, lon_local = cotangent.shape
     rows = fields * levels
-    grid_lat = lat_local * X * ZHI * CORE
-    _, hi, _, _, _ = place()
-    to_hi = (hi + jnp.array(GROUP_STEP)) % ZHI
-    plane = jnp.arange(PLANE)
-    slots = (to_hi * CORE * ZLO + jnp.array(GROUP_PLACE))[:, :, None] * Y + (
-        (plane // (CORE * Y) * ZHI * CORE + plane // Y % CORE) * ZLO * Y + plane % Y
-    )
-    coeffs = zonal_sums(cotangent.reshape(rows, lat_local, lon_local), wave_order[slots])
-    steps = coeffs.shape[0]
-    share = steps * ROWS
-    coeffs = coeffs.reshape(steps, ZHI, lat_local, ROWS, 2, PLANE)
-    blocks = coeffs.transpose(5, 4, 0, 3, 1, 2).reshape(PLANE, -1, 128)
-    gathered = plane_exchange(blocks).reshape(X * CORE, Y, 2, share, ZHI * lat_local)
-    gathered = gathered.transpose(2, 1, 3, 0, 4).reshape(2, Y * share, grid_lat)
-    spare = Y * share - rows
-    gathered = jnp.concatenate(
-        [gathered[:, : (Y - 1) * share], gathered[:, (Y - 1) * share + spare :]], axis=1
-    )
-    spectra = jnp.einsum(
-        "crn,nk->crk",
-        gathered,
-        meridional_table(grid_lat, lat_local),
-        preferred_element_type=jnp.float32,
-    ).astype(jnp.bfloat16)
-    block_count = band_diagonal.shape[1]
-    diagonal_blocks = band_diagonal[0].reshape(block_count, BLK, BLK)
-    lower_blocks = band_lower[0].reshape(block_count - 1, BLK, BLK)
-    blocks = spectra.reshape(2, rows, block_count, BLK)
-    banded = band_apply(blocks, diagonal_blocks, lower_blocks).astype(jnp.bfloat16)
-    layered = banded.reshape(2, fields, levels, grid_lat)
-    mixed = jnp.einsum(
-        "flm,cflk->cfmk", vertical_matrix, layered, preferred_element_type=jnp.float32
-    )
-    return mixed.astype(jnp.bfloat16)[None]
+    coeffs = zonal_sums(cotangent.reshape(rows, lat_local, lon_local), wave_order)
+    return finish(
+        coeffs, band_diagonal[0], band_lower[0], vertical_matrix, rows, lat_local * X * ZHI * CORE
+    )[None]
 
 
 def solution(mesh):

time: 186 us -> 136 us (0.73)
  local copies, waits for them, and re-layouts: 34.3 us -> 2.82 us
  other arithmetic: 7.47 us -> 0 us
  Pallas kernels: 139 us -> 133 us
  matrix products: 4.84 us -> 0 us
    reshape x6 -> x0, local copies, waits for them, and re-layouts: 14.2 us -> none  [the longest x1 6.34 us: per_device(): blocks = coeffs.transpose(5, 4, 0, 3, 1, 2).reshape(PLANE, -1, 128)]
    dot_general x5 -> x0, matrix products: 4.84 us -> none  [the longest x1 1.64 us: per_device(): jnp.einsum('crn,nk->crk', gathered, meridional_table(grid_lat, lat_local)...]
    transpose x2 -> x0, local copies, waits for them, and re-layouts: 4.1 us -> none  [the longest x1 3.39 us: per_device(): blocks = coeffs.transpose(5, 4, 0, 3, 1, 2).reshape(PLANE, -1, 128)]
    pallas_call x1, Pallas kernels: 32 us -> 28.4 us  [finish(): pl.pallas_call(functools.partial(mode_kernel, rows, share), out_shape=jax...]
    gather x2 -> x0, local copies, waits for them, and re-layouts: 3.57 us -> none  [per_device(): wave_order[slots]]
    another operation x3 -> x0, local copies, waits for them, and re-layouts: 3.32 us -> none  [the longest x2 2.19 us: per_device(): lower_blocks = band_lower[0].reshape(block_count - 1, BLK, BLK)]
    pallas_call x1, Pallas kernels: 107 us -> 104 us  [zonal_sums(): pl.pallas_call(functools.partial(zonal_kernel, rows, share, steps), out_s...]
    pallas_call x1 -> x0, local copies, waits for them, and re-layouts: 2.39 us -> none  [zonal_sums(): pl.pallas_call(functools.partial(zonal_kernel, rows, share, steps), out_s...]
where the time goes in v1:
time: 136 us
  Pallas kernels  133 us (98%)
  local copies, waits for them, and re-layouts  2.82 us (2%)
    pallas_call x1, Pallas kernels, zonal_sums(): pl.pallas_call(functools.partial(zonal_kernel, rows, share, steps), out_s...  104 us
    pallas_call x1, Pallas kernels, finish(): pl.pallas_call(functools.partial(mode_kernel, rows, share), out_shape=jax...  28.4 us

profile of v1, /device:TPU:1, one launch (start us, length us, event | category | flops | bytes accessed | tf_op | source)
XLA Modules:
  0.0 135.6 jit_solution(14017987594758021073)
XLA Ops:
  0.0 0.0 copy-start.3
  0.0 0.0 copy-start.2
  0.0 0.0 copy-start.1
  0.0 104.4 %shard_map.55.in_ref = bf16[19,4,48,128]{3,2,1,0:T(8,128)(2,1)} custom-call(bf16[150,48,256]{2,1,0:T(8,128)(2,1)} %bitcast.8, s32[1,512]{1,0:T(1,128)} %bitcast.9), custom_call_target="tpu_custom_call" | custom-call | tf_op jit(solution)/shard_map/pallas_call | solution.py:254
  104.4 0.0 copy-done.3
  104.4 0.0 copy-done.2
  104.4 0.0 copy-done.1
  104.4 0.0 copy-start
  104.4 1.2 copy-done
  105.6 28.4 %shard_map.56 = bf16[2,3,50,1536]{3,2,1,0:T(8,128)(2,1)S(1)} custom-call(bf16[19,4,48,128]{3,2,1,0:T(8,128)(2,1)S(1)} %copy-done, bf16[24,4096]{1,0:T(8,128)(2,1)S(1)} %bitcast.6, bf16[23,4096]{1,0:T(8,128)(2,1)S(1)} %bitcast.7, bf16[3,50,50]{2,1,0:T(8,128)(2,1)S(1)} %copy-done.3), custom_call_target="tpu_custom_call" | custom-call | tf_op jit(solution)/shard_map/pallas_call | solution.py:464
  134.0 1.6 %copy.6 = bf16[1,2,3,50,1536]{4,1,3,2,0:T(2,128)(2,1)} copy(bf16[1,2,3,50,1536]{4,3,2,1,0:T(8,128)(2,1)S(1)} %bitcast.5) | data formatting | bytes 1843200 | tf_op jit(solution)/shard_map/broadcast_in_dim | solution.py:498
Async XLA Ops:
  0.0 104.4 %copy-start.3 = (bf16[3,50,50]{2,1,0:T(8,128)(2,1)S(1)}, bf16[3,50,50]{2,1,0:T(8,128)(2,1)}, u32[]{:S(2)}) copy-start(bf16[3,50,50]{2,1,0:T(8,128)(2,1)} %vertical_ref.1) | copy-start | bytes 45004
  0.0 104.4 %copy-start.2 = (bf16[1,23,4096]{2,1,0:T(8,128)(2,1)S(1)}, bf16[1,23,4096]{2,1,0:T(8,128)(2,1)}, u32[]{:S(2)}) copy-start(bf16[1,23,4096]{2,1,0:T(8,128)(2,1)} %param.8) | copy-start | bytes 565252
  0.0 104.4 %copy-start.1 = (bf16[1,24,4096]{2,1,0:T(8,128)(2,1)S(1)}, bf16[1,24,4096]{2,1,0:T(8,128)(2,1)}, u32[]{:S(2)}) copy-start(bf16[1,24,4096]{2,1,0:T(8,128)(2,1)} %param.7) | copy-start | bytes 589828
  104.4 1.2 copy-start

commit v2 on v0

v2 whole, which is shorter than its diff:
```python
import functools
import math

import jax
import jax.numpy as jnp
from jax import lax
from jax.experimental import pallas as pl
from jax.experimental.pallas import tpu as pltpu
from jax.sharding import PartitionSpec as P

BLK = 64
MESH = pl.DeviceIdType.MESH

X, ZHI, CORE, ZLO, Y = 4, 4, 2, 4, 4
PLANE = X * CORE * Y
GROUP = 4
SIDES, DESTS = 2, 8
GROUP_STEP = ((3, 3, 3, 3, 2, 2, 0, 0), (1, 1, 1, 1, 2, 2, 0, 0))
GROUP_PLACE = ((0, 1, 2, 3, 2, 3, 0, 1), (0, 1, 2, 3, 0, 1, 2, 3))
ROWS = 2
AHEAD = 4
LAG = 3
COARSE = 32
SKEW = 2


def place():
    lat, lon = lax.axis_index("lat"), lax.axis_index("lon")
    return lat // (ZHI * CORE), lat // CORE % ZHI, lat % CORE, lon // Y, lon % Y


def device(x, hi, core, lo, y):
    return ((x * ZHI + hi) * CORE + core, lo * Y + y)


def cosine(phase, period):
    quarter = period // 4
    turns = jnp.floor(phase * (1.0 / quarter) + 0.5)
    angle = (phase - turns * quarter) * (2.0 * math.pi / period)
    square = angle * angle
    even = 1.0 + square * (
        -1 / 2 + square * (1 / 24 + square * (-1 / 720 + square * (1 / 40320)))
    )
    odd = angle * (
        1.0 + square * (-1 / 6 + square * (1 / 120 + square * (-1 / 5040 + square * (1 / 362880))))
    )
    turn = turns.astype(jnp.int32) & 3
    value = jnp.where((turn & 1) == 1, odd, even)
    return jnp.where((turn == 1) | (turn == 2), -value, value)


def slots_of_columns(hi, column):
    width = 2 * PLANE
    side, dest, plane = column // (DESTS * width), column // width % DESTS, column % PLANE
    step = jnp.where(dest < 4, jnp.where(side == 0, 3, 1), jnp.where(dest < 6, 2, 0))
    low_side = jnp.where(dest < 4, dest, jnp.where(dest < 6, dest - 2, dest - 6))
    lo = jnp.where(side == 0, low_side, dest % 4)
    lo = jnp.where((side == 1) & (dest >= 6), dest - 4, lo)
    to_hi = (hi + step) % ZHI
    x, core, y = plane // (CORE * Y), plane // Y % CORE, plane % Y
    return (((x * ZHI + to_hi) * CORE + core) * ZLO + lo) * Y + y


def waves_of_columns(wave_ref, hi, columns):
    slots = wave_ref.shape[1]
    slot = slots_of_columns(hi, lax.broadcasted_iota(jnp.int32, (1, columns), 1))
    wave = jnp.broadcast_to(wave_ref[...], (8, slots))
    pick = lax.broadcasted_iota(jnp.int32, (slots, columns), 0) == slot
    pick = jnp.where(pick, 1.0, 0.0).astype(jnp.bfloat16)

    def picked(digits):
        digits = digits.astype(jnp.float32).astype(jnp.bfloat16)
        return jnp.dot(digits, pick, preferred_element_type=jnp.float32)[:1]

    return picked(wave // 16) * 16.0 + picked(wave % 16)


def step_kernel(
    rows, share, steps,
    grid_ref, wave_ref, diagonal_ref, lower_ref, vertical_ref, out_ref,
    grid, basis, u_ref, v_ref, right_in, left_in, right_out, left_out, packed, total,
    parts, wide, spread, sending, gathered,
    table, base_cos, base_sin, near_cos, near_sin,
    diagonal, lower, band, levels_pad, mix, spectra, banded,
    grid_sem, grid_send, right_send, right_recv, left_send, left_recv,
    pack_send, part_sem, plane_send, plane_sem,
):
    x, hi, core, lo, y = place()
    mine = (x * CORE + core) * Y + y
    lat_local, lon_local = grid_ref.shape[1:]
    half = basis.shape[1] // 2
    width = half // DESTS
    f32, bf16 = jnp.float32, jnp.bfloat16

    def peer(offset):
        other = (mine + offset) % PLANE
        return other, device(other // (CORE * Y), hi, other // Y % CORE, lo, other % Y)

    barrier = pltpu.get_barrier_semaphore()

    def greet_line(offset, carry):
        z = (hi * ZLO + lo + offset) % (ZHI * ZLO)
        pl.semaphore_signal(
            barrier, inc=1, device_id=device(x, z // ZLO, core, z % ZLO, y), device_id_type=MESH
        )
        return carry

    def greet_plane(offset, carry):
        pl.semaphore_signal(barrier, inc=1, device_id=peer(offset)[1], device_id_type=MESH)
        return carry

    lax.fori_loop(1, ZHI * ZLO, greet_line, 0)
    lax.fori_loop(1, PLANE, greet_plane, 0)
    pl.semaphore_wait(barrier, ZHI * ZLO - 1 + PLANE - 1)

    def first_row(owner):
        return jnp.minimum(owner * share, rows - share)

    def grid_copies(step):
        columns = pl.ds(pl.multiple_of(y * lon_local, lon_local), lon_local)
        target = grid.at[pl.ds(step * ROWS, ROWS), :, columns]
        for offset in range(1, Y):
            owner = (y + offset) % Y
            pltpu.make_async_remote_copy(
                src_ref=grid_ref.at[pl.ds(first_row(owner) + step * ROWS, ROWS)],
                dst_ref=target,
                send_sem=grid_send,
                recv_sem=grid_sem.at[step],
                device_id=device(x, hi, core, lo, owner),
                device_id_type=MESH,
            ).start()
        pltpu.make_async_copy(
            grid_ref.at[pl.ds(first_row(y) + step * ROWS, ROWS)], target, grid_sem.at[step]
        ).start()

    for step in range(AHEAD):
        grid_copies(step)

    waves = waves_of_columns(wave_ref, hi, basis.shape[1])
    column = lax.broadcasted_iota(jnp.int32, (1, basis.shape[1]), 1)
    sine = jnp.where(column // PLANE % 2 == 1, 1.0, 0.0)
    lon, grid_lon = basis.shape[0], basis.shape[0] * ZLO
    coarse, fine = u_ref.shape[0], lon // u_ref.shape[0]
    scale = math.sqrt(2.0 / grid_lon)
    first = (lo * lon + fine * lax.broadcasted_iota(jnp.int32, (coarse, 1), 0)).astype(f32)
    base = waves * first - sine * (grid_lon // 4)
    u_ref[...] = cosine(base, grid_lon) * scale
    v_ref[...] = cosine(base + grid_lon // 4, grid_lon) * scale
    near = waves * lax.broadcasted_iota(jnp.int32, (fine, 1), 0).astype(f32)
    fine_cos, fine_sin = cosine(near, grid_lon), cosine(near - grid_lon // 4, grid_lon)

    def fill(a, carry):
        piece = u_ref[pl.ds(a, 1), :] * fine_cos + v_ref[pl.ds(a, 1), :] * fine_sin
        basis[pl.ds(pl.multiple_of(a * fine, fine), fine), :] = piece.astype(bf16)
        return carry

    lax.fori_loop(0, coarse, fill, 0)

    def product(step, side):
        left = grid[pl.ds(step * ROWS, ROWS)].reshape(ROWS * lat_local, grid.shape[2])
        return jnp.dot(
            left, basis[:, side * half : (side + 1) * half], preferred_element_type=f32
        )

    def hand_out(step, side):
        for pair in range(DESTS // 2):
            lanes = slice(pair * 2 * width, (pair + 1) * 2 * width)
            top, low = total[:lat_local, lanes], total[lat_local:, lanes]
            for odd in range(2):
                part = slice(odd * width, (odd + 1) * width)
                packed[step, pair * 2 + odd] = jnp.concatenate(
                    [top[:, part], low[:, part]], axis=1
                ).astype(bf16)
        own_lo = ZLO - 1 if side else 0
        for dest in range(DESTS):
            to_hi = (hi + GROUP_STEP[side][dest]) % ZHI
            to_lo = GROUP_PLACE[side][dest]
            if GROUP_STEP[side][dest] == 0 and to_lo == own_lo:
                pltpu.make_async_copy(
                    packed.at[step, dest], parts.at[step, hi], part_sem.at[step]
                ).start()
            else:
                pltpu.make_async_remote_copy(
                    src_ref=packed.at[step, dest],
                    dst_ref=parts.at[step, hi],
                    send_sem=pack_send,
                    recv_sem=part_sem.at[step],
                    device_id=device(x, to_hi, core, to_lo, y),
                    device_id_type=MESH,
                ).start()

    def chain(step, side):
        arrived, leaving = (right_in, right_out) if side else (left_in, left_out)
        send_sem, recv_sem = (right_send, right_recv) if side else (left_send, left_recv)
        first, last = (0, ZLO - 1) if side else (ZLO - 1, 0)
        total[...] = product(step, side)

        @pl.when(lo != first)
        def _():
            pltpu.make_async_copy(arrived.at[step], arrived.at[step], recv_sem.at[step]).wait()
            total[...] += arrived[step].astype(f32)

        @pl.when(lo != last)
        def _():
            leaving[step] = total[...].astype(bf16)
            pltpu.make_async_remote_copy(
                src_ref=leaving.at[step],
                dst_ref=arrived.at[step],
                send_sem=send_sem,
                recv_sem=recv_sem.at[step],
                device_id=device(x, hi, core, lo + (1 if side else -1), y),
                device_id_type=MESH,
            ).start()

        @pl.when(lo == last)
        def _():
            hand_out(step, side)

    span = ZHI * lat_local
    depth = sending.shape[1]
    tall = 4 * GROUP

    def turn(step):
        pltpu.make_async_copy(parts.at[step], parts.at[step], part_sem.at[step]).wait()
        wide[:span, :] = parts[step].reshape(span, 128).astype(f32)
        turned = wide[...].T
        for group in range(4):
            for part in range(2):
                spread[part, pl.ds(4 * step + group, PLANE, stride=depth), :] = turned[
                    group * PLANE : (group + 1) * PLANE, part * 128 : (part + 1) * 128
                ]

    def through_plane(group):
        at = pl.ds(pl.multiple_of(group * tall, tall), tall)

        def narrow(other, carry):
            begin = pl.multiple_of(other * depth + group * tall, tall)
            for part in range(2):
                sending[other, at, part * 128 : (part + 1) * 128] = spread[
                    part, pl.ds(begin, tall), :
                ].astype(bf16)
            return carry

        lax.fori_loop(0, PLANE, narrow, 0)

        def send(offset, carry):
            other, where = peer(offset)
            pltpu.make_async_remote_copy(
                src_ref=sending.at[other, at],
                dst_ref=gathered.at[mine, at],
                send_sem=plane_send,
                recv_sem=plane_sem.at[group],
                device_id=where,
                device_id_type=MESH,
            ).start()
            return carry

        lax.fori_loop(1, PLANE, send, 0)
        pltpu.make_async_copy(
            sending.at[mine, at], gathered.at[mine, at], plane_sem.at[group]
        ).start()

    grid_lat = table.shape[1]
    blocks = diagonal_ref.shape[0]
    fields, levels = vertical_ref.shape[:2]
    owners = X * ZHI * CORE
    pairs = blocks // 2

    def start_meridional():
        scale = math.sqrt(2.0 / grid_lat)
        mode = lax.broadcasted_iota(jnp.int32, (1, grid_lat), 1).astype(f32)
        base = 2 * lat_local * lax.broadcasted_iota(jnp.int32, (owners, 1), 0)
        base = base.astype(f32) * mode
        base_cos[...] = cosine(base, 4 * grid_lat) * scale
        base_sin[...] = cosine(base - grid_lat, 4 * grid_lat) * scale
        near = (2 * lax.broadcasted_iota(jnp.int32, (lat_local, 1), 0) + 1).astype(f32) * mode
        near_cos[...] = cosine(near, 4 * grid_lat)
        near_sin[...] = cosine(near - grid_lat, 4 * grid_lat)
        wide[...] = jnp.zeros_like(wide)
        for row in range(4 * steps, depth):
            for part in range(2):
                spread[part, pl.ds(row, PLANE, stride=depth), :] = jnp.zeros((PLANE, 128), f32)
        for source in range(X * CORE):
            table[source * 256 + span : (source + 1) * 256, :] = jnp.zeros(
                (256 - span, grid_lat), bf16
            )

    def meridional(owner):
        to_x, to_hi, to_core = owner // (ZHI * CORE), owner // CORE % ZHI, owner % CORE
        at = (to_x * CORE + to_core) * 256 + to_hi * lat_local
        piece = base_cos[pl.ds(owner, 1), :] * near_cos[...]
        piece -= base_sin[pl.ds(owner, 1), :] * near_sin[...]
        table[pl.ds(pl.multiple_of(at, 16), lat_local), :] = piece.astype(bf16)

    def squares(lanes):
        tile = pl.ds(pl.multiple_of(lanes * 128, 128), 128)
        for flat, square in ((diagonal_ref, diagonal), (lower_ref, lower)):
            piece = flat[:, tile].astype(f32)
            square[pl.ds(2 * lanes, flat.shape[0], stride=BLK), :] = piece
            square[pl.ds(2 * lanes + 1, flat.shape[0], stride=BLK), :] = pltpu.roll(piece, 64, 1)

    def square(ref, block):
        return ref[pl.ds(pl.multiple_of(block * BLK, BLK), BLK), :][:, :BLK]

    def band_pair(pair):
        one, two = 2 * pair, 2 * pair + 1
        empty = jnp.zeros((BLK, BLK), f32)
        before = jnp.where(pair > 0, square(lower, jnp.maximum(one - 1, 0)), 0.0)
        after = square(lower, jnp.minimum(two, blocks - 2)).T
        after = jnp.where(two < blocks - 1, after, 0.0)
        inner = square(lower, one)
        top = (empty, before, square(diagonal, one), inner.T, empty, empty)
        low = (empty, empty, inner, square(diagonal, two), after, empty)
        band[pair, :BLK, :] = jnp.concatenate(top, axis=1).astype(bf16)
        band[pair, BLK:, :] = jnp.concatenate(low, axis=1).astype(bf16)

    held = mix.shape[1]

    def mixing():
        at = lax.broadcasted_iota(jnp.int32, (1, held), 1)
        owner, within = at // depth, at % depth
        row = jnp.minimum(owner * share, rows - share) + within // 2
        fresh = (row >= owner * share) & (within < 2 * share)
        level = lax.broadcasted_iota(jnp.int32, (BLK, 1), 0)
        for field in range(fields):
            levels_pad[...] = jnp.zeros_like(levels_pad)
            levels_pad[:levels, :levels] = vertical_ref[field].astype(f32)
            turned = levels_pad[...].T[:BLK, :].astype(bf16)
            pick = (row == field * levels + level) & (level < levels) & fresh
            pick = jnp.where(pick, 1.0, 0.0).astype(bf16)
            pick = jnp.concatenate([pick, jnp.zeros((128 - BLK, held), bf16)], axis=0)
            mixed = jnp.dot(turned, pick, preferred_element_type=f32)
            for c in range(2):
                part = (c * fields + field) * BLK
                mix[part : part + BLK, :] = jnp.where(at % 2 == c, mixed, 0.0).astype(bf16)

    count = steps + SKEW * (ZLO - 1) + LAG
    duties = (
        (start_meridional, 1, 1, 0),
        (mixing, 2, 1, 0),
        (squares, 3, BLK // 2, 2),
        (meridional, 2, owners, 2),
        (band_pair, 3 + BLK // 4, pairs, 2),
    )

    def one(step, carry):
        @pl.when(step + AHEAD < steps)
        def _():
            grid_copies(step + AHEAD)

        first = step - SKEW * jnp.minimum(lo, ZLO - 1 - lo)

        @pl.when((first >= 0) & (first < steps))
        def _():
            block = grid.at[pl.ds(first * ROWS, ROWS)]
            pltpu.make_async_copy(block, block, grid_sem.at[first]).wait()

        for side in range(SIDES):
            at = step - SKEW * (lo if side else ZLO - 1 - lo)

            @pl.when((at >= 0) & (at < steps))
            def _():
                chain(at, side)

        done = step - SKEW * (ZLO - 1) - LAG

        @pl.when(done >= 0)
        def _():
            turn(done)

        @pl.when((done >= 0) & ((done % GROUP == GROUP - 1) | (done == steps - 1)))
        def _():
            through_plane(done // GROUP)

        for duty, begin, number, each in duties:
            if each:

                @pl.when((step >= begin) & (step < begin + number // each))
                def _():
                    for extra in range(each):
                        duty((step - begin) * each + extra)
            else:

                @pl.when(step == begin)
                def _():
                    duty()

        return carry

    lax.fori_loop(0, count, one, 0)

    sent = grid_ref.at[pl.ds(0, (Y - 1) * share)]
    pltpu.make_async_copy(sent, sent, grid_send).wait()

    @pl.when(lo != ZLO - 1)
    def _():
        pltpu.make_async_copy(right_out, right_out, right_send).wait()

    @pl.when(lo != 0)
    def _():
        pltpu.make_async_copy(left_out, left_out, left_send).wait()

    @pl.when((lo == 0) | (lo == ZLO - 1))
    def _():
        sent = packed.at[:, pl.ds(0, DESTS - 1)]
        pltpu.make_async_copy(sent, sent, pack_send).wait()

    groups = depth // tall
    for begin, end in ((0, groups - 1), (groups - 1, groups)):
        for group in range(begin, end):
            block = gathered.at[:, pl.ds(group * tall, tall)]
            pltpu.make_async_copy(block, block, plane_sem.at[group]).wait()
        at = slice(begin * tall, end * tall)
        high = Y * (end - begin) * tall
        left = jnp.concatenate(
            [
                gathered[source * Y : (source + 1) * Y, at].reshape(high, 256)
                for source in range(X * CORE)
            ],
            axis=1,
        )
        for tile in range(grid_lat // 512):
            lanes = slice(tile * 512, (tile + 1) * 512)
            term = jnp.dot(left, table[:, lanes], preferred_element_type=f32)
            spectra[:, at, lanes] = term.astype(bf16).reshape(Y, (end - begin) * tall, 512)
        for pair in range(pairs):
            low, top = max(0, pair - 1) * 128, min(pairs, pair + 2) * 128
            skip = 0 if pair else 128
            banded[:, at, pair * 128 : (pair + 1) * 128] = (
                lax.dot_general(
                    spectra[:, at, low:top].reshape(high, top - low),
                    band[pair, :, skip : skip + top - low],
                    (((1,), (1,)), ((), ())),
                    preferred_element_type=f32,
                )
                .astype(bf16)
                .reshape(Y, (end - begin) * tall, 128)
            )

    sent = sending.at[pl.ds(0, PLANE - 1)]
    pltpu.make_async_copy(sent, sent, plane_send).wait()

    for tile in range(grid_lat // 512):
        lanes = slice(tile * 512, (tile + 1) * 512)
        result = jnp.dot(
            mix[...], banded[:, :, lanes].reshape(held, 512), preferred_element_type=f32
        )
        for c in range(2):
            for field in range(fields):
                at = (c * fields + field) * BLK
                out_ref[c, field, :, lanes] = result[at : at + levels].astype(out_ref.dtype)


def per_device(cotangent, wave_order, band_diagonal, band_lower, vertical_matrix):
    fields, levels, lat_local, lon_local = cotangent.shape
    rows = fields * levels
    grid_lat = lat_local * X * ZHI * CORE
    lon = lon_local * Y
    share = -(-rows // (Y * ROWS)) * ROWS
    steps = share // ROWS
    columns = 2 * wave_order.size
    half = columns // 2
    packed = (lat_local, ROWS * half // DESTS)
    tall = 4 * GROUP
    depth = -(-2 * share // tall) * tall
    owners = X * ZHI * CORE
    blocks = band_diagonal.shape[1]
    f32, bf16 = jnp.float32, jnp.bfloat16
    chain = pltpu.VMEM((steps, ROWS * lat_local, half), bf16)
    hbm = pl.BlockSpec(memory_space=pl.ANY)
    vmem = pl.BlockSpec(memory_space=pltpu.VMEM)
    dma = pltpu.SemaphoreType.DMA
    return pl.pallas_call(
        functools.partial(step_kernel, rows, share, steps),
        out_shape=jax.ShapeDtypeStruct((2, fields, levels, grid_lat), bf16),
        in_specs=[hbm] + [vmem] * 4,
        out_specs=vmem,
        scratch_shapes=[
            pltpu.VMEM((share, lat_local, lon), bf16),
            pltpu.VMEM((lon, columns), bf16),
            pltpu.VMEM((COARSE, columns), f32),
            pltpu.VMEM((COARSE, columns), f32),
            chain,
            chain,
            chain,
            chain,
            pltpu.VMEM((steps, DESTS) + packed, bf16),
            pltpu.VMEM((ROWS * lat_local, half), f32),
            pltpu.VMEM((steps, ZHI) + packed, bf16),
            pltpu.VMEM((256, 128), f32),
            pltpu.VMEM((2, PLANE * depth, 128), f32),
            pltpu.VMEM((PLANE, depth, 256), bf16),
            pltpu.VMEM((PLANE, depth, 256), bf16),
            pltpu.VMEM((X * CORE * 256, grid_lat), bf16),
            pltpu.VMEM((owners, grid_lat), f32),
            pltpu.VMEM((owners, grid_lat), f32),
            pltpu.VMEM((lat_local, grid_lat), f32),
            pltpu.VMEM((lat_local, grid_lat), f32),
            pltpu.VMEM((blocks * BLK, 128), f32),
            pltpu.VMEM(((blocks - 1) * BLK, 128), f32),
            pltpu.VMEM((blocks // 2, 2 * BLK, 6 * BLK), bf16),
            pltpu.VMEM((128, 128), f32),
            pltpu.VMEM((2 * fields * BLK, Y * depth), bf16),
            pltpu.VMEM((Y, depth, grid_lat), bf16),
            pltpu.VMEM((Y, depth, grid_lat), bf16),
            dma((steps,)),
            dma,
            dma,
            dma((steps,)),
            dma,
            dma((steps,)),
            dma,
            dma((steps,)),
            dma,
            dma((depth // tall,)),
        ],
        compiler_params=pltpu.CompilerParams(
            collective_id=0, has_side_effects=True, vmem_limit_bytes=61 << 20
        ),
    )(
        cotangent.reshape(rows, lat_local, lon_local),
        wave_order.reshape(1, -1),
        band_diagonal[0],
        band_lower[0],
        vertical_matrix,
    )[None]


def solution(mesh):
    return jax.shard_map(
        per_device,
        mesh=mesh,
        in_specs=(
            P(None, None, "lat", "lon"),
            P(),
            P(("lat", "lon"), None, None),
            P(("lat", "lon"), None, None),
            P(),
        ),
        out_specs=P(("lat", "lon"), None, None, None, None),
        check_vma=False,
    )
```

time: 186 us -> 123 us (0.66)
  local copies, waits for them, and re-layouts: 34.3 us -> 2.85 us
  Pallas kernels: 139 us -> 120 us
  other arithmetic: 7.47 us -> 0 us
  matrix products: 4.84 us -> 0 us
    pallas_call x2 -> x1, Pallas kernels: 139 us -> 120 us  [per_device(): pl.pallas_call(functools.partial(step_kernel, rows, share, steps), out_sh...]
    reshape x6 -> x0, local copies, waits for them, and re-layouts: 14.2 us -> none  [the longest x1 6.34 us: per_device(): blocks = coeffs.transpose(5, 4, 0, 3, 1, 2).reshape(PLANE, -1, 128)]
    dot_general x5 -> x0, matrix products: 4.84 us -> none  [the longest x1 1.64 us: per_device(): jnp.einsum('crn,nk->crk', gathered, meridional_table(grid_lat, lat_local)...]
    transpose x2 -> x0, local copies, waits for them, and re-layouts: 4.1 us -> none  [the longest x1 3.39 us: per_device(): blocks = coeffs.transpose(5, 4, 0, 3, 1, 2).reshape(PLANE, -1, 128)]
    gather x2 -> x0, local copies, waits for them, and re-layouts: 3.57 us -> none  [per_device(): wave_order[slots]]
    another operation x3 -> x0, local copies, waits for them, and re-layouts: 3.32 us -> none  [the longest x2 2.19 us: per_device(): lower_blocks = band_lower[0].reshape(block_count - 1, BLK, BLK)]
    unnamed x22 -> x0, local copies, waits for them, and re-layouts: 2.52 us -> none
    pallas_call x1 -> x0, local copies, waits for them, and re-layouts: 2.39 us -> none  [zonal_sums(): pl.pallas_call(functools.partial(zonal_kernel, rows, share, steps), out_s...]
where the time goes in v2:
time: 123 us
  Pallas kernels  120 us (98%)
  local copies, waits for them, and re-layouts  2.85 us (2%)
    pallas_call x1, Pallas kernels, per_device(): pl.pallas_call(functools.partial(step_kernel, rows, share, steps), out_sh...  120 us
    broadcast_in_dim x1, local copies, waits for them, and re-layouts, per_device(): pl.pallas_call(functools.partial(step_kernel, rows, share, steps), out_sh...  2.85 us

profile of v2, /device:TPU:1, one launch (start us, length us, event | category | flops | bytes accessed | tf_op | source)
XLA Modules:
  0.0 123.3 jit_solution(9934614684083425003)
XLA Ops:
  0.0 120.4 %shard_map.55 = bf16[2,3,50,1536]{3,2,1,0:T(8,128)(2,1)} custom-call(bf16[150,48,256]{2,1,0:T(8,128)(2,1)} %bitcast.6, s32[1,512]{1,0:T(1,128)} %bitcast.9, bf16[24,4096]{1,0:T(8,128)(2,1)} %bitcast.7, bf16[23,4096]{1,0:T(8,128)(2,1)} %bitcast.8, bf16[3,50,50]{2,1,0:T(8,128)(2,1)} %vertical_ref.1), custom_call_target="tpu_custom_call" | custom-call | tf_op jit(solution)/shard_map/pallas_call | solution.py:473
  120.4 2.9 %copy.6 = bf16[1,2,3,50,1536]{4,1,3,2,0:T(2,128)(2,1)} copy(bf16[1,2,3,50,1536]{4,3,2,1,0:T(8,128)(2,1)} %bitcast.5) | data formatting | bytes 1843200 | tf_op jit(solution)/shard_map/broadcast_in_dim | solution.py:473

commit v3 on v2

--- a/solution.py
+++ b/solution.py
@@ -18,10 +18,11 @@
 GROUP_STEP = ((3, 3, 3, 3, 2, 2, 0, 0), (1, 1, 1, 1, 2, 2, 0, 0))
 GROUP_PLACE = ((0, 1, 2, 3, 2, 3, 0, 1), (0, 1, 2, 3, 0, 1, 2, 3))
 ROWS = 2
-AHEAD = 4
-LAG = 3
+FIRST = 2
+AHEAD = 2
+LAG = 4
 COARSE = 32
-SKEW = 2
+SKEW = 3
 
 
 def place():
@@ -81,7 +82,7 @@
     grid, basis, u_ref, v_ref, right_in, left_in, right_out, left_out, packed, total,
     parts, wide, spread, sending, gathered,
     table, base_cos, base_sin, near_cos, near_sin,
-    diagonal, lower, band, levels_pad, mix, spectra, banded,
+    diagonal, lower, band, levels_pad, mix, spectra, banded, mixed_early,
     grid_sem, grid_send, right_send, right_recv, left_send, left_recv,
     pack_send, part_sem, plane_send, plane_sem,
 ):
@@ -133,7 +134,7 @@
             grid_ref.at[pl.ds(first_row(y) + step * ROWS, ROWS)], target, grid_sem.at[step]
         ).start()
 
-    for step in range(AHEAD):
+    for step in range(FIRST):
         grid_copies(step)
 
     waves = waves_of_columns(wave_ref, hi, basis.shape[1])
@@ -155,6 +156,8 @@
         return carry
 
     lax.fori_loop(0, coarse, fill, 0)
+    for step in range(FIRST, AHEAD):
+        grid_copies(step)
 
     def product(step, side):
         left = grid[pl.ds(step * ROWS, ROWS)].reshape(ROWS * lat_local, grid.shape[2])
@@ -165,7 +168,7 @@
     def hand_out(step, side):
         for pair in range(DESTS // 2):
             lanes = slice(pair * 2 * width, (pair + 1) * 2 * width)
-            top, low = total[:lat_local, lanes], total[lat_local:, lanes]
+            top, low = total[side, :lat_local, lanes], total[side, lat_local:, lanes]
             for odd in range(2):
                 part = slice(odd * width, (odd + 1) * width)
                 packed[step, pair * 2 + odd] = jnp.concatenate(
@@ -193,16 +196,21 @@
         arrived, leaving = (right_in, right_out) if side else (left_in, left_out)
         send_sem, recv_sem = (right_send, right_recv) if side else (left_send, left_recv)
         first, last = (0, ZLO - 1) if side else (ZLO - 1, 0)
-        total[...] = product(step, side)
+        row = step % ROWS
+        sums = total.at[side, pl.ds(pl.multiple_of(row * lat_local, lat_local), lat_local)]
+
+        @pl.when(row == 0)
+        def _():
+            total[side] = product(step // ROWS, side)
 
         @pl.when(lo != first)
         def _():
             pltpu.make_async_copy(arrived.at[step], arrived.at[step], recv_sem.at[step]).wait()
-            total[...] += arrived[step].astype(f32)
+            sums[...] += arrived[step].astype(f32)
 
         @pl.when(lo != last)
         def _():
-            leaving[step] = total[...].astype(bf16)
+            leaving[step] = sums[...].astype(bf16)
             pltpu.make_async_remote_copy(
                 src_ref=leaving.at[step],
                 dst_ref=arrived.at[step],
@@ -212,9 +220,9 @@
                 device_id_type=MESH,
             ).start()
 
-        @pl.when(lo == last)
-        def _():
-            hand_out(step, side)
+        @pl.when((lo == last) & (row == ROWS - 1))
+        def _():
+            hand_out(step // ROWS, side)
 
     span = ZHI * lat_local
     depth = sending.shape[1]
@@ -233,18 +241,16 @@
     def through_plane(group):
         at = pl.ds(pl.multiple_of(group * tall, tall), tall)
 
-        def narrow(other, carry):
+        def narrow(other):
             begin = pl.multiple_of(other * depth + group * tall, tall)
             for part in range(2):
                 sending[other, at, part * 128 : (part + 1) * 128] = spread[
                     part, pl.ds(begin, tall), :
                 ].astype(bf16)
-            return carry
-
-        lax.fori_loop(0, PLANE, narrow, 0)
 
         def send(offset, carry):
             other, where = peer(offset)
+            narrow(other)
             pltpu.make_async_remote_copy(
                 src_ref=sending.at[other, at],
                 dst_ref=gathered.at[mine, at],
@@ -256,6 +262,7 @@
             return carry
 
         lax.fori_loop(1, PLANE, send, 0)
+        narrow(mine)
         pltpu.make_async_copy(
             sending.at[mine, at], gathered.at[mine, at], plane_sem.at[group]
         ).start()
@@ -315,10 +322,13 @@
         band[pair, BLK:, :] = jnp.concatenate(low, axis=1).astype(bf16)
 
     held = mix.shape[1]
+    early = depth - tall
 
     def mixing():
         at = lax.broadcasted_iota(jnp.int32, (1, held), 1)
-        owner, within = at // depth, at % depth
+        rest = at - Y * early
+        owner = jnp.where(rest < 0, at // early, rest // tall)
+        within = jnp.where(rest < 0, at % early, early + rest % tall)
         row = jnp.minimum(owner * share, rows - share) + within // 2
         fresh = (row >= owner * share) & (within < 2 * share)
         level = lax.broadcasted_iota(jnp.int32, (BLK, 1), 0)
@@ -334,43 +344,45 @@
                 part = (c * fields + field) * BLK
                 mix[part : part + BLK, :] = jnp.where(at % 2 == c, mixed, 0.0).astype(bf16)
 
-    count = steps + SKEW * (ZLO - 1) + LAG
+    fill_steps = SKEW * (ZLO - 1)
+    count = (steps + LAG) * ROWS + fill_steps
     duties = (
-        (start_meridional, 1, 1, 0),
-        (mixing, 2, 1, 0),
-        (squares, 3, BLK // 2, 2),
-        (meridional, 2, owners, 2),
-        (band_pair, 3 + BLK // 4, pairs, 2),
+        (start_meridional, 10, 1, 0),
+        (mixing, 11, 1, 0),
+        (squares, 12, BLK // 2, 2),
+        (meridional, 11, owners, 1),
+        (band_pair, 12 + BLK // 4, pairs, 1),
     )
 
     def one(step, carry):
-        @pl.when(step + AHEAD < steps)
-        def _():
-            grid_copies(step + AHEAD)
+        @pl.when((step % ROWS == 0) & (step // ROWS + AHEAD < steps))
+        def _():
+            grid_copies(step // ROWS + AHEAD)
 
         first = step - SKEW * jnp.minimum(lo, ZLO - 1 - lo)
 
-        @pl.when((first >= 0) & (first < steps))
-        def _():
-            block = grid.at[pl.ds(first * ROWS, ROWS)]
-            pltpu.make_async_copy(block, block, grid_sem.at[first]).wait()
-
-        for side in range(SIDES):
+        @pl.when((first >= 0) & (first < steps * ROWS) & (first % ROWS == 0))
+        def _():
+            block = grid.at[pl.ds(first, ROWS)]
+            pltpu.make_async_copy(block, block, grid_sem.at[first // ROWS]).wait()
+
+        for side, here in ((1, lo < ZLO // 2), (0, lo >= 0), (1, lo >= ZLO // 2)):
             at = step - SKEW * (lo if side else ZLO - 1 - lo)
 
-            @pl.when((at >= 0) & (at < steps))
+            @pl.when(here & (at >= 0) & (at < steps * ROWS))
             def _():
                 chain(at, side)
 
-        done = step - SKEW * (ZLO - 1) - LAG
-
-        @pl.when(done >= 0)
+        ahead = step - fill_steps - (ROWS - 1) - LAG * ROWS
+        done = ahead // ROWS
+
+        @pl.when((ahead >= 0) & (ahead % ROWS == 0))
         def _():
             turn(done)
 
-        @pl.when((done >= 0) & ((done % GROUP == GROUP - 1) | (done == steps - 1)))
-        def _():
-            through_plane(done // GROUP)
+            @pl.when((done % GROUP == GROUP - 1) | (done == steps - 1))
+            def _():
+                through_plane(done // GROUP)
 
         for duty, begin, number, each in duties:
             if each:
@@ -410,11 +422,11 @@
         for group in range(begin, end):
             block = gathered.at[:, pl.ds(group * tall, tall)]
             pltpu.make_async_copy(block, block, plane_sem.at[group]).wait()
-        at = slice(begin * tall, end * tall)
         high = Y * (end - begin) * tall
+        at = slice(Y * begin * tall, Y * end * tall)
         left = jnp.concatenate(
             [
-                gathered[source * Y : (source + 1) * Y, at].reshape(high, 256)
+                gathered[source * Y : (source + 1) * Y, begin * tall : end * tall].reshape(high, 256)
                 for source in range(X * CORE)
             ],
             axis=1,
@@ -422,33 +434,30 @@
         for tile in range(grid_lat // 512):
             lanes = slice(tile * 512, (tile + 1) * 512)
             term = jnp.dot(left, table[:, lanes], preferred_element_type=f32)
-            spectra[:, at, lanes] = term.astype(bf16).reshape(Y, (end - begin) * tall, 512)
+            spectra[at, lanes] = term.astype(bf16)
         for pair in range(pairs):
             low, top = max(0, pair - 1) * 128, min(pairs, pair + 2) * 128
             skip = 0 if pair else 128
-            banded[:, at, pair * 128 : (pair + 1) * 128] = (
-                lax.dot_general(
-                    spectra[:, at, low:top].reshape(high, top - low),
-                    band[pair, :, skip : skip + top - low],
-                    (((1,), (1,)), ((), ())),
-                    preferred_element_type=f32,
-                )
-                .astype(bf16)
-                .reshape(Y, (end - begin) * tall, 128)
-            )
+            banded[at, pair * 128 : (pair + 1) * 128] = lax.dot_general(
+                spectra[at, low:top],
+                band[pair, :, skip : skip + top - low],
+                (((1,), (1,)), ((), ())),
+                preferred_element_type=f32,
+            ).astype(bf16)
+        for tile in range(grid_lat // 512):
+            lanes = slice(tile * 512, (tile + 1) * 512)
+            result = jnp.dot(mix[:, at], banded[at, lanes], preferred_element_type=f32)
+            if begin == 0:
+                mixed_early[:, lanes] = result
+                continue
+            result += mixed_early[:, lanes]
+            for c in range(2):
+                for field in range(fields):
+                    row = (c * fields + field) * BLK
+                    out_ref[c, field, :, lanes] = result[row : row + levels].astype(out_ref.dtype)
 
     sent = sending.at[pl.ds(0, PLANE - 1)]
     pltpu.make_async_copy(sent, sent, plane_send).wait()
-
-    for tile in range(grid_lat // 512):
-        lanes = slice(tile * 512, (tile + 1) * 512)
-        result = jnp.dot(
-            mix[...], banded[:, :, lanes].reshape(held, 512), preferred_element_type=f32
-        )
-        for c in range(2):
-            for field in range(fields):
-                at = (c * fields + field) * BLK
-                out_ref[c, field, :, lanes] = result[at : at + levels].astype(out_ref.dtype)
 
 
 def per_device(cotangent, wave_order, band_diagonal, band_lower, vertical_matrix):
@@ -466,7 +475,7 @@
     owners = X * ZHI * CORE
     blocks = band_diagonal.shape[1]
     f32, bf16 = jnp.float32, jnp.bfloat16
-    chain = pltpu.VMEM((steps, ROWS * lat_local, half), bf16)
+    chain = pltpu.VMEM((steps * ROWS, lat_local, half), bf16)
     hbm = pl.BlockSpec(memory_space=pl.ANY)
     vmem = pl.BlockSpec(memory_space=pltpu.VMEM)
     dma = pltpu.SemaphoreType.DMA
@@ -485,7 +494,7 @@
             chain,
             chain,
             pltpu.VMEM((steps, DESTS) + packed, bf16),
-            pltpu.VMEM((ROWS * lat_local, half), f32),
+            pltpu.VMEM((SIDES, ROWS * lat_local, half), f32),
             pltpu.VMEM((steps, ZHI) + packed, bf16),
             pltpu.VMEM((256, 128), f32),
             pltpu.VMEM((2, PLANE * depth, 128), f32),
@@ -501,21 +510,22 @@
             pltpu.VMEM((blocks // 2, 2 * BLK, 6 * BLK), bf16),
             pltpu.VMEM((128, 128), f32),
             pltpu.VMEM((2 * fields * BLK, Y * depth), bf16),
-            pltpu.VMEM((Y, depth, grid_lat), bf16),
-            pltpu.VMEM((Y, depth, grid_lat), bf16),
+            pltpu.VMEM((Y * depth, grid_lat), bf16),
+            pltpu.VMEM((Y * depth, grid_lat), bf16),
+            pltpu.VMEM((2 * fields * BLK, grid_lat), f32),
             dma((steps,)),
             dma,
             dma,
-            dma((steps,)),
+            dma((steps * ROWS,)),
             dma,
-            dma((steps,)),
+            dma((steps * ROWS,)),
             dma,
             dma((steps,)),
             dma,
             dma((depth // tall,)),
         ],
         compiler_params=pltpu.CompilerParams(
-            collective_id=0, has_side_effects=True, vmem_limit_bytes=61 << 20
+            collective_id=0, has_side_effects=True, vmem_limit_bytes=52 << 20
         ),
     )(
         cotangent.reshape(rows, lat_local, lon_local),

time: 123 us -> 120 us (0.976)
  Pallas kernels: 120 us -> 115 us
  local copies, waits for them, and re-layouts: 2.85 us -> 4.95 us
    pallas_call x1, Pallas kernels: 120 us -> 115 us  [per_device(): pl.pallas_call(functools.partial(step_kernel, rows, share, steps), out_sh...]
    unnamed x0 -> x8, local copies, waits for them, and re-layouts: none -> 3.32 us
where the time goes in v3:
time: 120 us
  Pallas kernels  115 us (96%)
  local copies, waits for them, and re-layouts  4.95 us (4%)
    pallas_call x1, Pallas kernels, per_device(): pl.pallas_call(functools.partial(step_kernel, rows, share, steps), out_sh...  115 us
    unnamed x8, local copies, waits for them, and re-layouts  3.32 us

profile of v3, /device:TPU:1, one launch (start us, length us, event | category | flops | bytes accessed | tf_op | source)
XLA Modules:
  0.0 120.0 jit_solution(13603858614304998740)
XLA Ops:
  0.0 0.0 copy-start
  0.0 0.9 copy-done
  0.9 0.0 copy-start.1
  0.9 0.9 copy-done.1
  1.9 0.0 copy-start.2
  1.9 0.8 copy-done.2
  2.6 0.0 copy-start.3
  2.6 0.7 copy-done.3
  3.3 115.1 %shard_map.55 = bf16[2,3,50,1536]{3,2,1,0:T(8,128)(2,1)S(1)} custom-call(bf16[150,48,256]{2,1,0:T(8,128)(2,1)} %bitcast.9, s32[1,512]{1,0:T(1,128)S(1)} %bitcast.8, bf16[24,4096]{1,0:T(8,128)(2,1)S(1)} %bitcast.6, bf16[23,4096]{1,0:T(8,128)(2,1)S(1)} %bitcast.7, bf16[3,50,50]{2,1,0:T(8,128)(2,1)S(1)} %copy-done.2), custom_call_target="tpu_custom_call" | custom-call | tf_op jit(solution)/shard_map/pallas_call | solution.py:482
  118.4 1.6 %copy.6 = bf16[1,2,3,50,1536]{4,1,3,2,0:T(2,128)(2,1)} copy(bf16[1,2,3,50,1536]{4,3,2,1,0:T(8,128)(2,1)S(1)} %bitcast.5) | data formatting | bytes 1843200 | tf_op jit(solution)/shard_map/broadcast_in_dim | solution.py:482
Async XLA Ops:
  0.0 0.9 copy-start
  0.9 0.9 copy-start.1
  1.9 0.8 copy-start.2
  2.6 0.7 copy-start.3

commit v4 on v3

--- a/solution.py
+++ b/solution.py
@@ -78,13 +78,14 @@
 
 def step_kernel(
     rows, share, steps,
-    grid_ref, wave_ref, diagonal_ref, lower_ref, vertical_ref, out_ref,
+    grid_ref, wave_hbm, diagonal_hbm, lower_hbm, vertical_hbm, out_ref,
+    wave_ref, diagonal_ref, lower_ref, vertical_ref,
     grid, basis, u_ref, v_ref, right_in, left_in, right_out, left_out, packed, total,
     parts, wide, spread, sending, gathered,
     table, base_cos, base_sin, near_cos, near_sin,
     diagonal, lower, band, levels_pad, mix, spectra, banded, mixed_early,
     grid_sem, grid_send, right_send, right_recv, left_send, left_recv,
-    pack_send, part_sem, plane_send, plane_sem,
+    pack_send, part_sem, plane_send, plane_sem, own_sem,
 ):
     x, hi, core, lo, y = place()
     mine = (x * CORE + core) * Y + y
@@ -97,6 +98,17 @@
         other = (mine + offset) % PLANE
         return other, device(other // (CORE * Y), hi, other // Y % CORE, lo, other % Y)
 
+    own = [
+        pltpu.make_async_copy(there, here, own_sem.at[number])
+        for number, (there, here) in enumerate(
+            (
+                (wave_hbm, wave_ref),
+                (diagonal_hbm, diagonal_ref),
+                (lower_hbm, lower_ref),
+                (vertical_hbm, vertical_ref),
+            )
+        )
+    ]
     barrier = pltpu.get_barrier_semaphore()
 
     def greet_line(offset, carry):
@@ -112,6 +124,8 @@
 
     lax.fori_loop(1, ZHI * ZLO, greet_line, 0)
     lax.fori_loop(1, PLANE, greet_plane, 0)
+    for copy in own:
+        copy.start()
     pl.semaphore_wait(barrier, ZHI * ZLO - 1 + PLANE - 1)
 
     def first_row(owner):
@@ -137,6 +151,7 @@
     for step in range(FIRST):
         grid_copies(step)
 
+    own[0].wait()
     waves = waves_of_columns(wave_ref, hi, basis.shape[1])
     column = lax.broadcasted_iota(jnp.int32, (1, basis.shape[1]), 1)
     sine = jnp.where(column // PLANE % 2 == 1, 1.0, 0.0)
@@ -156,6 +171,8 @@
         return carry
 
     lax.fori_loop(0, coarse, fill, 0)
+    for copy in own[1:]:
+        copy.wait()
     for step in range(FIRST, AHEAD):
         grid_copies(step)
 
@@ -481,10 +498,14 @@
     dma = pltpu.SemaphoreType.DMA
     return pl.pallas_call(
         functools.partial(step_kernel, rows, share, steps),
-        out_shape=jax.ShapeDtypeStruct((2, fields, levels, grid_lat), bf16),
-        in_specs=[hbm] + [vmem] * 4,
+        out_shape=pltpu.VMEM((2, fields, levels, grid_lat), bf16),
+        in_specs=[hbm] * 5,
         out_specs=vmem,
         scratch_shapes=[
+            pltpu.VMEM((1, wave_order.size), jnp.int32),
+            pltpu.VMEM(band_diagonal.shape[1:], bf16),
+            pltpu.VMEM(band_lower.shape[1:], bf16),
+            pltpu.VMEM(vertical_matrix.shape, bf16),
             pltpu.VMEM((share, lat_local, lon), bf16),
             pltpu.VMEM((lon, columns), bf16),
             pltpu.VMEM((COARSE, columns), f32),
@@ -523,9 +544,10 @@
             dma((steps,)),
             dma,
             dma((depth // tall,)),
+            dma((4,)),
         ],
         compiler_params=pltpu.CompilerParams(
-            collective_id=0, has_side_effects=True, vmem_limit_bytes=52 << 20
+            collective_id=0, has_side_effects=True, vmem_limit_bytes=54 << 20
         ),
     )(
         cotangent.reshape(rows, lat_local, lon_local),

time: 120 us -> 117 us (0.975)
  local copies, waits for them, and re-layouts: 4.95 us -> 1.64 us
    unnamed x8 -> x0, local copies, waits for them, and re-layouts: 3.32 us -> none
where the time goes in v4:
time: 117 us
  Pallas kernels  116 us (99%)
  local copies, waits for them, and re-layouts  1.64 us (1%)
    pallas_call x1, Pallas kernels, per_device(): pl.pallas_call(functools.partial(step_kernel, rows, share, steps), out_sh...  116 us

profile of v4, /device:TPU:1, one launch (start us, length us, event | category | flops | bytes accessed | tf_op | source)
XLA Modules:
  0.0 117.3 jit_solution(15001177131711225849)
XLA Ops:
  0.0 115.6 %shard_map.55 = bf16[2,3,50,1536]{3,2,1,0:T(8,128)(2,1)S(1)} custom-call(bf16[150,48,256]{2,1,0:T(8,128)(2,1)} %bitcast.6, s32[1,512]{1,0:T(1,128)} %bitcast.9, bf16[24,4096]{1,0:T(8,128)(2,1)} %bitcast.7, bf16[23,4096]{1,0:T(8,128)(2,1)} %bitcast.8, bf16[3,50,50]{2,1,0:T(8,128)(2,1)} %vertical_hbm.1), custom_call_target="tpu_custom_call" | custom-call | tf_op jit(solution)/shard_map/pallas_call | solution.py:499
  115.7 1.6 %copy.6 = bf16[1,2,3,50,1536]{4,1,3,2,0:T(2,128)(2,1)} copy(bf16[1,2,3,50,1536]{4,3,2,1,0:T(8,128)(2,1)S(1)} %bitcast.5) | data formatting | bytes 1843200 | tf_op jit(solution)/shard_map/broadcast_in_dim | solution.py:499

commit v5 on v4

--- a/solution.py
+++ b/solution.py
@@ -83,7 +83,7 @@
     grid, basis, u_ref, v_ref, right_in, left_in, right_out, left_out, packed, total,
     parts, wide, spread, sending, gathered,
     table, base_cos, base_sin, near_cos, near_sin,
-    diagonal, lower, band, levels_pad, mix, spectra, banded, mixed_early,
+    diagonal, lower, band, levels_pad, mix, spectra, banded, mixed_early, late,
     grid_sem, grid_send, right_send, right_recv, left_send, left_recv,
     pack_send, part_sem, plane_send, plane_sem, own_sem,
 ):
@@ -255,6 +255,13 @@
                     group * PLANE : (group + 1) * PLANE, part * 128 : (part + 1) * 128
                 ]
 
+    groups = depth // tall
+
+    def arrival(group, offset):
+        other = (mine + offset) % PLANE
+        across = (other // (CORE * Y) + X - x) % X * CORE + (other // Y % CORE + CORE - core) % CORE
+        return plane_sem.at[group + group // (groups - 1) * across]
+
     def through_plane(group):
         at = pl.ds(pl.multiple_of(group * tall, tall), tall)
 
@@ -272,7 +279,7 @@
                 src_ref=sending.at[other, at],
                 dst_ref=gathered.at[mine, at],
                 send_sem=plane_send,
-                recv_sem=plane_sem.at[group],
+                recv_sem=arrival(group, offset),
                 device_id=where,
                 device_id_type=MESH,
             ).start()
@@ -281,7 +288,7 @@
         lax.fori_loop(1, PLANE, send, 0)
         narrow(mine)
         pltpu.make_async_copy(
-            sending.at[mine, at], gathered.at[mine, at], plane_sem.at[group]
+            sending.at[mine, at], gathered.at[mine, at], arrival(group, 0)
         ).start()
 
     grid_lat = table.shape[1]
@@ -434,24 +441,40 @@
         sent = packed.at[:, pl.ds(0, DESTS - 1)]
         pltpu.make_async_copy(sent, sent, pack_send).wait()
 
-    groups = depth // tall
     for begin, end in ((0, groups - 1), (groups - 1, groups)):
-        for group in range(begin, end):
-            block = gathered.at[:, pl.ds(group * tall, tall)]
-            pltpu.make_async_copy(block, block, plane_sem.at[group]).wait()
         high = Y * (end - begin) * tall
         at = slice(Y * begin * tall, Y * end * tall)
-        left = jnp.concatenate(
-            [
-                gathered[source * Y : (source + 1) * Y, begin * tall : end * tall].reshape(high, 256)
-                for source in range(X * CORE)
-            ],
-            axis=1,
-        )
-        for tile in range(grid_lat // 512):
-            lanes = slice(tile * 512, (tile + 1) * 512)
-            term = jnp.dot(left, table[:, lanes], preferred_element_type=f32)
-            spectra[at, lanes] = term.astype(bf16)
+        if begin == 0:
+            for group in range(begin, end):
+                block = gathered.at[:, pl.ds(group * tall, tall)]
+                pltpu.make_async_copy(block, block, plane_sem.at[group]).wait()
+            left = jnp.concatenate(
+                [
+                    gathered[source * Y : (source + 1) * Y, : end * tall].reshape(high, 256)
+                    for source in range(X * CORE)
+                ],
+                axis=1,
+            )
+            for tile in range(grid_lat // 512):
+                lanes = slice(tile * 512, (tile + 1) * 512)
+                term = jnp.dot(left, table[:, lanes], preferred_element_type=f32)
+                spectra[at, lanes] = term.astype(bf16)
+        else:
+            for across in (0, 1, 2, 3, 6, 7, 4, 5):
+                source = (x + X - across // CORE) % X * CORE + (core + CORE - across % CORE) % CORE
+                part = pl.ds(source * Y, Y)
+                block = gathered.at[part, pl.ds(begin * tall, tall)]
+                pltpu.make_async_copy(block, block, plane_sem.at[begin + across]).wait()
+                left = gathered[part, begin * tall : end * tall].reshape(high, 256)
+                right = pl.ds(pl.multiple_of(source * 256, 256), 256)
+                for tile in range(grid_lat // 512):
+                    lanes = slice(tile * 512, (tile + 1) * 512)
+                    term = jnp.dot(left, table[right, lanes], preferred_element_type=f32)
+                    if across == 0:
+                        late[:, lanes] = term
+                    else:
+                        late[:, lanes] += term
+            spectra[at, :] = late[...].astype(bf16)
         for pair in range(pairs):
             low, top = max(0, pair - 1) * 128, min(pairs, pair + 2) * 128
             skip = 0 if pair else 128
@@ -534,6 +557,7 @@
             pltpu.VMEM((Y * depth, grid_lat), bf16),
             pltpu.VMEM((Y * depth, grid_lat), bf16),
             pltpu.VMEM((2 * fields * BLK, grid_lat), f32),
+            pltpu.VMEM((Y * tall, grid_lat), f32),
             dma((steps,)),
             dma,
             dma,
@@ -543,7 +567,7 @@
             dma,
             dma((steps,)),
             dma,
-            dma((depth // tall,)),
+            dma((depth // tall - 1 + X * CORE,)),
             dma((4,)),
         ],
         compiler_params=pltpu.CompilerParams(

time: 117 us -> 117 us (level)
  no operation moved by 1% of the time
where the time goes in v5:
time: 117 us
  Pallas kernels  115 us (98%)
  local copies, waits for them, and re-layouts  1.64 us (1%)
    pallas_call x1, Pallas kernels, per_device(): pl.pallas_call(functools.partial(step_kernel, rows, share, steps), out_sh...  115 us

profile of v5, /device:TPU:1, one launch (start us, length us, event | category | flops | bytes accessed | tf_op | source)
XLA Modules:
  0.0 116.7 jit_solution(4299657456609309580)
XLA Ops:
  0.0 115.1 %shard_map.55 = bf16[2,3,50,1536]{3,2,1,0:T(8,128)(2,1)S(1)} custom-call(bf16[150,48,256]{2,1,0:T(8,128)(2,1)} %bitcast.6, s32[1,512]{1,0:T(1,128)} %bitcast.9, bf16[24,4096]{1,0:T(8,128)(2,1)} %bitcast.7, bf16[23,4096]{1,0:T(8,128)(2,1)} %bitcast.8, bf16[3,50,50]{2,1,0:T(8,128)(2,1)} %vertical_hbm.1), custom_call_target="tpu_custom_call" | custom-call | tf_op jit(solution)/shard_map/pallas_call | solution.py:522
  115.1 1.6 %copy.6 = bf16[1,2,3,50,1536]{4,1,3,2,0:T(2,128)(2,1)} copy(bf16[1,2,3,50,1536]{4,3,2,1,0:T(8,128)(2,1)S(1)} %bitcast.5) | data formatting | bytes 1843200 | tf_op jit(solution)/shard_map/broadcast_in_dim | solution.py:522

commit v6 on v5

--- a/solution.py
+++ b/solution.py
@@ -550,7 +550,7 @@
             pltpu.VMEM((lat_local, grid_lat), f32),
             pltpu.VMEM((lat_local, grid_lat), f32),
             pltpu.VMEM((blocks * BLK, 128), f32),
-            pltpu.VMEM(((blocks - 1) * BLK, 128), f32),
+            pltpu.VMEM((blocks * BLK, 128), f32),
             pltpu.VMEM((blocks // 2, 2 * BLK, 6 * BLK), bf16),
             pltpu.VMEM((128, 128), f32),
             pltpu.VMEM((2 * fields * BLK, Y * depth), bf16),

time: 117 us -> 117 us (level)
  no operation moved by 1% of the time
where the time goes in v6:
time: 117 us
  Pallas kernels  115 us (98%)
  local copies, waits for them, and re-layouts  1.64 us (1%)
    pallas_call x1, Pallas kernels, per_device(): pl.pallas_call(functools.partial(step_kernel, rows, share, steps), out_sh...  115 us

profile of v6, /device:TPU:1, one launch (start us, length us, event | category | flops | bytes accessed | tf_op | source)
XLA Modules:
  0.0 116.7 jit_solution(8967958949848880229)
XLA Ops:
  0.0 115.1 %shard_map.55 = bf16[2,3,50,1536]{3,2,1,0:T(8,128)(2,1)S(1)} custom-call(bf16[150,48,256]{2,1,0:T(8,128)(2,1)} %bitcast.6, s32[1,512]{1,0:T(1,128)} %bitcast.9, bf16[24,4096]{1,0:T(8,128)(2,1)} %bitcast.7, bf16[23,4096]{1,0:T(8,128)(2,1)} %bitcast.8, bf16[3,50,50]{2,1,0:T(8,128)(2,1)} %vertical_hbm.1), custom_call_target="tpu_custom_call" | custom-call | tf_op jit(solution)/shard_map/pallas_call | solution.py:522
  115.1 1.6 %copy.6 = bf16[1,2,3,50,1536]{4,1,3,2,0:T(2,128)(2,1)} copy(bf16[1,2,3,50,1536]{4,3,2,1,0:T(8,128)(2,1)S(1)} %bitcast.5) | data formatting | bytes 1843200 | tf_op jit(solution)/shard_map/broadcast_in_dim | solution.py:522
